TPU v7x, 256 devices: a whole 4x4x8 slice. The times are simulated.
256 devices in a mesh: outer: 16 (over y_hi, z), inner: 16 (over y_lo, x, core).
Axes of the slice: x: 4, y: 4 (y_hi: 2, y_lo: 2; y = y_hi * 2 + y_lo), z: 8, core: 2. Of those that a mesh axis runs over, the one named last changes fastest.
Arguments:
- queries: bfloat16 [131072, 1024], P(('outer', 'inner')), may hold values from -4.5 to 4.5
- keys: bfloat16 [131072, 128], P(('outer', 'inner')), may hold values from -4.5 to 4.5
- values: bfloat16 [131072, 128], P(('outer', 'inner')), may hold values from -6 to 6
- key_blocks: int32 [1024, 44], P(('outer', 'inner')), may hold values from 0 to 1023, as said below
- key_counts: int32 [1024], P(('outer', 'inner')), may hold values from 4 to 44, as said below
Outputs:
- context: bfloat16 [131072, 1024], P(('outer', 'inner'))
Inputs may be any that keep to these rules, and one draw needn't show every extreme that they name: `key_blocks`: row b lists 44 blocks, the live ones distinct, b itself first; all lie in group b // 64 or in the two groups beside it on the closed cycle of 16 groups; entries from key_counts[b] onward equal b. `key_counts`: some row lists 44 live entries.
All inputs are finite; a program needn't handle non-finite values.
Results may differ from a plain program's by a relative error of at most 0.0047.
Values may be sent and summed in bfloat16 or wider, within the bound.
A program may use at most 128 MiB of HBM per device.

v0:
```python
import jax
import jax.numpy as jnp
from jax import lax
from jax.sharding import PartitionSpec as P

HD = 128
HEADS = 8
BLOCK = 128
MAXB = 44


def shifted(block, axis, distance):
    devices = range(lax.axis_size(axis))
    route = [((i - distance) % len(devices), i) for i in devices]
    return lax.ppermute(block, axis, route)


def body(queries, keys, values, key_blocks, key_counts):
    groups = lax.axis_size("outer")
    blocks_here = keys.shape[0] // BLOCK
    group_blocks = blocks_here * lax.axis_size("inner")
    kv_shard = jnp.concatenate([keys, values], axis=1)
    group_set = lax.all_gather(kv_shard, "inner", axis=0, tiled=True)
    before_set = shifted(group_set, "outer", 1)
    later_set = shifted(group_set, "outer", -1)
    window = jnp.concatenate([before_set, group_set, later_set], axis=0)
    window = window.reshape(3 * group_blocks, BLOCK, 2 * HD)
    own_group = lax.axis_index("outer")
    key_group = key_blocks // group_blocks
    local_index = (
        key_group - own_group + 1 + groups
    ) % groups * group_blocks + key_blocks % group_blocks
    query_tiles = queries.reshape(blocks_here, BLOCK, HEADS, HD)

    def attend_block(items):
        query_block, block_list, live_count = items
        picked = jnp.take(window, block_list, axis=0).reshape(MAXB * BLOCK, 2 * HD)
        key_rows = picked[:, :HD]
        value_rows = picked[:, HD:]
        scores = jnp.einsum(
            "qhd,kd->hqk", query_block, key_rows, preferred_element_type=jnp.float32
        ) * HD ** (-0.5)
        live_mask = jnp.arange(MAXB * BLOCK, dtype=jnp.int32) // BLOCK < live_count
        scores = jnp.where(live_mask[None, None, :], scores, -jnp.inf)
        peak = jnp.max(scores, axis=2, keepdims=True)
        weights = jnp.exp(scores - peak)
        total = jnp.sum(weights, axis=2, keepdims=True)
        rounded = weights.astype(jnp.bfloat16)
        mixed_rows = (
            jnp.einsum("hqk,kd->hqd", rounded, value_rows, preferred_element_type=jnp.float32)
            / total
        )
        return jnp.transpose(mixed_rows, (1, 0, 2)).reshape(BLOCK, HEADS * HD).astype(jnp.bfloat16)

    result = lax.map(attend_block, (query_tiles, local_index, key_counts))
    return result.reshape(blocks_here * BLOCK, HEADS * HD)


def solution(mesh):
    placed = (
        P(("outer", "inner"), None),
        P(("outer", "inner"), None),
        P(("outer", "inner"), None),
        P(("outer", "inner"), None),
        P(("outer", "inner")),
    )
    return jax.shard_map(
        body, mesh=mesh, in_specs=placed, out_specs=P(("outer", "inner"), None), check_vma=False
    )
```

profile of v0, /device:TPU:1, one launch (start us, length us, event | category | flops | bytes accessed | tf_op | source)
XLA Modules:
  0.0 348.7 jit_solution(12664765170689693183)
XLA Ops:
  6.5 1.7 pad_maximum_fusion.1
  8.2 0.0 all-gather.2.cloned.1.call-update
  8.3 45.1 %all-gather.2.cloned.1.call-done = bf16[8192,256]{1,0:T(8,128)(2,1)} async-done(((bf16[512,256]{1,0:T(8,128)(2,1)}), bf16[8192,256]{1,0:T(8,128)(2,1)}) %all-gather.2.cloned.1.call-update) | async-done | bytes 4194320 | tf_op jit(solution)/shard_map/all_gather | solution.py:23
  53.3 1.3 collective-permute-start
  54.6 3.9 %collective-permute-start.1 = (bf16[8192,256]{1,0:T(8,128)(2,1)}, bf16[8192,256]{1,0:T(8,128)(2,1)}, u32[]{:S(2)}, u32[]{:S(2)}) collective-permute-start(bf16[8192,256]{1,0:T(8,128)(2,1)} %all-gather.2.cloned.1.call-done), channel_id=1, source_target_pairs={{16,0},{32,16},{48,32},{64,48},{80,64},{96,80},{112,96},{128,112},... | collective-permute-start | bytes 12582920 | tf_op jit(solution)/shard_map/ppermute | solution.py:15
  58.5 2.5 copy.19
  61.0 0.7 fusion.27
  61.7 87.7 %collective-permute-done = bf16[8192,256]{1,0:T(8,128)(2,1)} collective-permute-done((bf16[8192,256]{1,0:T(8,128)(2,1)}, bf16[8192,256]{1,0:T(8,128)(2,1)}, u32[]{:S(2)}, u32[]{:S(2)}) %collective-permute-start) | collective-permute-done | bytes 4194336 | tf_op jit(solution)/shard_map/ppermute | solution.py:15
  149.4 0.0 collective-permute-done.1
  149.4 15.4 %pad_maximum_fusion = bf16[24576,256]{1,0:T(8,128)(2,1)} fusion(bf16[8192,256]{1,0:T(8,128)(2,1)} %collective-permute-done.1, bf16[8192,256]{1,0:T(8,128)(2,1)} %all-gather.2.cloned.1.call-done, bf16[8192,256]{1,0:T(8,128)(2,1)} %collective-permute-done), kind=kLoop, calls=%fused_computation.36 | loop fusion | flops 37748736 | bytes 25165824 | tf_op jit(solution)/shard_map/concatenate | solution.py:26
  164.8 177.0 %while.12 = (s32[]{:T(128)}, bf16[4,128,1024]{2,1,0:T(8,128)(2,1)}, s32[4]{0:T(128)S(1)}, s32[4,44]{1,0:T(4,128)S(1)}, bf16[192,128,256]{2,1,0:T(8,128)(2,1)}, /*index=5*/bf16[4,128,8,128]{3,2,1,0:T(8,128)(2,1)}, s32[]{:T(128)}) while((s32[]{:T(128)}, bf16[4,128,1024]{2,1,0:T(8,128)(2,1)}, s32[4]{0:T(128)S(1)}, s32[4,44]{1,0:T(4,128)S(1)}, ...), condition=%wide.region_3.4_spmd, body=%wide.region_0.3_spmd.sunk | while | flops 3017982976 | bytes 189590640 | solution.py:55
  164.9 5.3 %gather_fusion = bf16[44,128,256]{2,1,0:T(8,128)(2,1)S(1)} fusion(bf16[192,128,256]{2,1,0:T(8,128)(2,1)} %get-tuple-element.163, s32[1024]{0:T(1024)S(1)} %pad_clamp_fusion.2), kind=kCustom, calls=%fused_computation.clone.1 | custom fusion | bytes 5767344 | tf_op jit(solution)/shard_map/while/body/eval_jaxpr/jit(_take)/gather | solution.py:37
  170.2 0.1 broadcast_bitcast_fusion.2
  170.3 3.8 %bitcast_select_fusion.2 = bf16[5632,256]{1,0:T(8,128)(2,1)} fusion(bf16[44,128,256]{2,1,0:T(8,128)(2,1)S(1)} %gather_fusion, pred[5632]{0:T(1024)(128)(4,1)S(1)} %broadcast_bitcast_fusion.2), kind=kLoop, calls=%fused_computation.9.clone.1 | loop fusion | flops 1441792 | bytes 5772800 | tf_op jit(solution)/shard_map/while/body/eval_jaxpr/jit(_take)/select_n | solution.py:37
  174.1 0.6 dynamic_slice.34
  174.6 0.6 fusion.36
  175.3 1.0 constant_dynamic-slice_fusion.3
  176.3 5.7 %bitcast_reduce_fusion.2 = (f32[8,128]{1,0:T(8,128)S(1)}, f32[5632,128,8]{1,0,2:T(8,128)S(1)}) fusion(pred[5632]{0:T(1024)(128)(4,1)S(1)} %fusion.36, bf16[1,128,8,128]{3,2,1,0:T(8,128)(2,1)S(1)} %constant_dynamic-slice_fusion.3, bf16[5632,256]{1,0:T(8,128)(2,1)} %bitcast_select_fusion.2), kind=kOutput, calls=%fused_computation.2.clone.1 | convolution fusion | flops 1493695488 | bytes 24782336 | tf_op jit(solution)/shard_map/while/body/eval_jaxpr/qhd,kd->hqk/dot_general | solution.py:40
  182.0 8.6 %copy-done = f32[5632,128,8]{1,0,2:T(8,128)} copy-done((f32[5632,128,8]{1,0,2:T(8,128)}, f32[5632,128,8]{1,0,2:T(8,128)S(1)}, u32[]{:S(2)}) %copy-start) | copy-done | bytes 23068696 | tf_op jit(solution)/shard_map/while
  190.6 6.4 %fusion.37 = f32[8,128]{1,0:T(8,128)S(1)} fusion(f32[5632,128,8]{1,0,2:T(8,128)S(1)} %get-tuple-element.143, f32[8,128]{1,0:T(8,128)S(1)} %get-tuple-element.144, pred[5632]{0:T(1024)(128)(4,1)S(1)} %fusion.36), kind=kLoop, calls=%fused_computation.5.clone.1 | loop fusion | flops 23067648 | bytes 23082496 | tf_op jit(solution)/shard_map/while/body/eval_jaxpr/reduce_sum | solution.py:47
  197.0 0.0 copy-done.1
  197.0 11.2 %fusion.38 = bf16[128,8,128]{0,2,1:T(8,128)(2,1)S(1)} fusion(bf16[5632,256]{1,0:T(8,128)(2,1)S(1)} %copy-done.1, f32[5632,128,8]{1,0,2:T(8,128)} %copy-done, f32[8,128]{1,0:T(8,128)S(1)} %get-tuple-element.144, pred[5632]{0:T(1024)(128)(4,1)S(1)} %fusion.36, f32[128,8]{0,1:T(8,128)S(1)} %bitcast.93), kind=kOutput, calls=%fused_computation.15.clone.1 | convolution fusion | flops 1499725824 | bytes 24786944 | tf_op jit(solution)/shard_map/while/body/eval_jaxpr/hqk,kd->hqd/dot_general | solution.py:50
  208.2 0.1 copy.27
  208.4 0.7 constant_dynamic-update-slice_fusion.2
  209.1 5.3 %gather_fusion = bf16[44,128,256]{2,1,0:T(8,128)(2,1)S(1)} fusion(bf16[192,128,256]{2,1,0:T(8,128)(2,1)} %get-tuple-element.163, s32[1024]{0:T(1024)S(1)} %pad_clamp_fusion.2), kind=kCustom, calls=%fused_computation.clone.1 | custom fusion | bytes 5767344 | tf_op jit(solution)/shard_map/while/body/eval_jaxpr/jit(_take)/gather | solution.py:37
  214.5 0.1 broadcast_bitcast_fusion.2
  214.5 3.8 %bitcast_select_fusion.2 = bf16[5632,256]{1,0:T(8,128)(2,1)} fusion(bf16[44,128,256]{2,1,0:T(8,128)(2,1)S(1)} %gather_fusion, pred[5632]{0:T(1024)(128)(4,1)S(1)} %broadcast_bitcast_fusion.2), kind=kLoop, calls=%fused_computation.9.clone.1 | loop fusion | flops 1441792 | bytes 5772800 | tf_op jit(solution)/shard_map/while/body/eval_jaxpr/jit(_take)/select_n | solution.py:37
  218.3 0.6 dynamic_slice.34
  218.9 0.6 fusion.36
  219.5 1.0 constant_dynamic-slice_fusion.3
  220.5 5.7 %bitcast_reduce_fusion.2 = (f32[8,128]{1,0:T(8,128)S(1)}, f32[5632,128,8]{1,0,2:T(8,128)S(1)}) fusion(pred[5632]{0:T(1024)(128)(4,1)S(1)} %fusion.36, bf16[1,128,8,128]{3,2,1,0:T(8,128)(2,1)S(1)} %constant_dynamic-slice_fusion.3, bf16[5632,256]{1,0:T(8,128)(2,1)} %bitcast_select_fusion.2), kind=kOutput, calls=%fused_computation.2.clone.1 | convolution fusion | flops 1493695488 | bytes 24782336 | tf_op jit(solution)/shard_map/while/body/eval_jaxpr/qhd,kd->hqk/dot_general | solution.py:40
  226.2 0.0 copy-start
  226.2 0.0 copy-start.1
  226.2 8.6 %copy-done = f32[5632,128,8]{1,0,2:T(8,128)} copy-done((f32[5632,128,8]{1,0,2:T(8,128)}, f32[5632,128,8]{1,0,2:T(8,128)S(1)}, u32[]{:S(2)}) %copy-start) | copy-done | bytes 23068696 | tf_op jit(solution)/shard_map/while
  234.8 6.4 %fusion.37 = f32[8,128]{1,0:T(8,128)S(1)} fusion(f32[5632,128,8]{1,0,2:T(8,128)S(1)} %get-tuple-element.143, f32[8,128]{1,0:T(8,128)S(1)} %get-tuple-element.144, pred[5632]{0:T(1024)(128)(4,1)S(1)} %fusion.36), kind=kLoop, calls=%fused_computation.5.clone.1 | loop fusion | flops 23067648 | bytes 23082496 | tf_op jit(solution)/shard_map/while/body/eval_jaxpr/reduce_sum | solution.py:47
  241.2 11.2 %fusion.38 = bf16[128,8,128]{0,2,1:T(8,128)(2,1)S(1)} fusion(bf16[5632,256]{1,0:T(8,128)(2,1)S(1)} %copy-done.1, f32[5632,128,8]{1,0,2:T(8,128)} %copy-done, f32[8,128]{1,0:T(8,128)S(1)} %get-tuple-element.144, pred[5632]{0:T(1024)(128)(4,1)S(1)} %fusion.36, f32[128,8]{0,1:T(8,128)S(1)} %bitcast.93), kind=kOutput, calls=%fused_computation.15.clone.1 | convolution fusion | flops 1499725824 | bytes 24786944 | tf_op jit(solution)/shard_map/while/body/eval_jaxpr/hqk,kd->hqd/dot_general | solution.py:50
  252.5 0.1 copy.27
  252.6 0.7 constant_dynamic-update-slice_fusion.2
  253.4 5.3 %gather_fusion = bf16[44,128,256]{2,1,0:T(8,128)(2,1)S(1)} fusion(bf16[192,128,256]{2,1,0:T(8,128)(2,1)} %get-tuple-element.163, s32[1024]{0:T(1024)S(1)} %pad_clamp_fusion.2), kind=kCustom, calls=%fused_computation.clone.1 | custom fusion | bytes 5767344 | tf_op jit(solution)/shard_map/while/body/eval_jaxpr/jit(_take)/gather | solution.py:37
  258.7 0.1 broadcast_bitcast_fusion.2
  258.8 3.8 %bitcast_select_fusion.2 = bf16[5632,256]{1,0:T(8,128)(2,1)} fusion(bf16[44,128,256]{2,1,0:T(8,128)(2,1)S(1)} %gather_fusion, pred[5632]{0:T(1024)(128)(4,1)S(1)} %broadcast_bitcast_fusion.2), kind=kLoop, calls=%fused_computation.9.clone.1 | loop fusion | flops 1441792 | bytes 5772800 | tf_op jit(solution)/shard_map/while/body/eval_jaxpr/jit(_take)/select_n | solution.py:37
  262.5 0.6 dynamic_slice.34
  263.1 0.6 fusion.36
  263.8 1.0 constant_dynamic-slice_fusion.3
  264.7 5.7 %bitcast_reduce_fusion.2 = (f32[8,128]{1,0:T(8,128)S(1)}, f32[5632,128,8]{1,0,2:T(8,128)S(1)}) fusion(pred[5632]{0:T(1024)(128)(4,1)S(1)} %fusion.36, bf16[1,128,8,128]{3,2,1,0:T(8,128)(2,1)S(1)} %constant_dynamic-slice_fusion.3, bf16[5632,256]{1,0:T(8,128)(2,1)} %bitcast_select_fusion.2), kind=kOutput, calls=%fused_computation.2.clone.1 | convolution fusion | flops 1493695488 | bytes 24782336 | tf_op jit(solution)/shard_map/while/body/eval_jaxpr/qhd,kd->hqk/dot_general | solution.py:40
  270.4 8.6 %copy-done = f32[5632,128,8]{1,0,2:T(8,128)} copy-done((f32[5632,128,8]{1,0,2:T(8,128)}, f32[5632,128,8]{1,0,2:T(8,128)S(1)}, u32[]{:S(2)}) %copy-start) | copy-done | bytes 23068696 | tf_op jit(solution)/shard_map/while
  279.1 6.4 %fusion.37 = f32[8,128]{1,0:T(8,128)S(1)} fusion(f32[5632,128,8]{1,0,2:T(8,128)S(1)} %get-tuple-element.143, f32[8,128]{1,0:T(8,128)S(1)} %get-tuple-element.144, pred[5632]{0:T(1024)(128)(4,1)S(1)} %fusion.36), kind=kLoop, calls=%fused_computation.5.clone.1 | loop fusion | flops 23067648 | bytes 23082496 | tf_op jit(solution)/shard_map/while/body/eval_jaxpr/reduce_sum | solution.py:47
  285.4 0.0 copy-done.1
  285.5 11.2 %fusion.38 = bf16[128,8,128]{0,2,1:T(8,128)(2,1)S(1)} fusion(bf16[5632,256]{1,0:T(8,128)(2,1)S(1)} %copy-done.1, f32[5632,128,8]{1,0,2:T(8,128)} %copy-done, f32[8,128]{1,0:T(8,128)S(1)} %get-tuple-element.144, pred[5632]{0:T(1024)(128)(4,1)S(1)} %fusion.36, f32[128,8]{0,1:T(8,128)S(1)} %bitcast.93), kind=kOutput, calls=%fused_computation.15.clone.1 | convolution fusion | flops 1499725824 | bytes 24786944 | tf_op jit(solution)/shard_map/while/body/eval_jaxpr/hqk,kd->hqd/dot_general | solution.py:50
  296.7 0.1 copy.27
  296.9 0.7 constant_dynamic-update-slice_fusion.2
  297.6 5.3 %gather_fusion = bf16[44,128,256]{2,1,0:T(8,128)(2,1)S(1)} fusion(bf16[192,128,256]{2,1,0:T(8,128)(2,1)} %get-tuple-element.163, s32[1024]{0:T(1024)S(1)} %pad_clamp_fusion.2), kind=kCustom, calls=%fused_computation.clone.1 | custom fusion | bytes 5767344 | tf_op jit(solution)/shard_map/while/body/eval_jaxpr/jit(_take)/gather | solution.py:37
  302.9 0.1 broadcast_bitcast_fusion.2
  303.0 3.8 %bitcast_select_fusion.2 = bf16[5632,256]{1,0:T(8,128)(2,1)} fusion(bf16[44,128,256]{2,1,0:T(8,128)(2,1)S(1)} %gather_fusion, pred[5632]{0:T(1024)(128)(4,1)S(1)} %broadcast_bitcast_fusion.2), kind=kLoop, calls=%fused_computation.9.clone.1 | loop fusion | flops 1441792 | bytes 5772800 | tf_op jit(solution)/shard_map/while/body/eval_jaxpr/jit(_take)/select_n | solution.py:37
  306.8 0.6 dynamic_slice.34
  307.4 0.6 fusion.36
  308.0 1.0 constant_dynamic-slice_fusion.3
  309.0 5.7 %bitcast_reduce_fusion.2 = (f32[8,128]{1,0:T(8,128)S(1)}, f32[5632,128,8]{1,0,2:T(8,128)S(1)}) fusion(pred[5632]{0:T(1024)(128)(4,1)S(1)} %fusion.36, bf16[1,128,8,128]{3,2,1,0:T(8,128)(2,1)S(1)} %constant_dynamic-slice_fusion.3, bf16[5632,256]{1,0:T(8,128)(2,1)} %bitcast_select_fusion.2), kind=kOutput, calls=%fused_computation.2.clone.1 | convolution fusion | flops 1493695488 | bytes 24782336 | tf_op jit(solution)/shard_map/while/body/eval_jaxpr/qhd,kd->hqk/dot_general | solution.py:40
  314.7 0.0 copy-start
  314.7 8.6 %copy-done = f32[5632,128,8]{1,0,2:T(8,128)} copy-done((f32[5632,128,8]{1,0,2:T(8,128)}, f32[5632,128,8]{1,0,2:T(8,128)S(1)}, u32[]{:S(2)}) %copy-start) | copy-done | bytes 23068696 | tf_op jit(solution)/shard_map/while
  323.3 6.4 %fusion.37 = f32[8,128]{1,0:T(8,128)S(1)} fusion(f32[5632,128,8]{1,0,2:T(8,128)S(1)} %get-tuple-element.143, f32[8,128]{1,0:T(8,128)S(1)} %get-tuple-element.144, pred[5632]{0:T(1024)(128)(4,1)S(1)} %fusion.36), kind=kLoop, calls=%fused_computation.5.clone.1 | loop fusion | flops 23067648 | bytes 23082496 | tf_op jit(solution)/shard_map/while/body/eval_jaxpr/reduce_sum | solution.py:47
  329.7 11.2 %fusion.38 = bf16[128,8,128]{0,2,1:T(8,128)(2,1)S(1)} fusion(bf16[5632,256]{1,0:T(8,128)(2,1)S(1)} %copy-done.1, f32[5632,128,8]{1,0,2:T(8,128)} %copy-done, f32[8,128]{1,0:T(8,128)S(1)} %get-tuple-element.144, pred[5632]{0:T(1024)(128)(4,1)S(1)} %fusion.36, f32[128,8]{0,1:T(8,128)S(1)} %bitcast.93), kind=kOutput, calls=%fused_computation.15.clone.1 | convolution fusion | flops 1499725824 | bytes 24786944 | tf_op jit(solution)/shard_map/while/body/eval_jaxpr/hqk,kd->hqd/dot_general | solution.py:50
  340.9 0.1 copy.27
  341.1 0.7 constant_dynamic-update-slice_fusion.2
  (23 shorter events, 0.1 us)
Async XLA Ops:
  6.5 46.8 %all-gather.2.cloned.1.call-start = ((), (), s32[]{:S(2)}) async-start(), calls=%async_computation | async-start | bytes 4456448 | tf_op jit(solution)/shard_map/all_gather | solution.py:23
  53.3 96.1 %collective-permute-start = (bf16[8192,256]{1,0:T(8,128)(2,1)}, bf16[8192,256]{1,0:T(8,128)(2,1)}, u32[]{:S(2)}, u32[]{:S(2)}) collective-permute-start(bf16[8192,256]{1,0:T(8,128)(2,1)} %all-gather.2.cloned.1.call-done), channel_id=1, source_target_pairs={{240,0},{0,16},{16,32},{32,48},{48,64},{64,80},{80,96},{96,112},{1... | collective-permute-start | bytes 12582920 | tf_op jit(solution)/shard_map/ppermute | solution.py:15
  54.6 94.8 %collective-permute-start.1 = (bf16[8192,256]{1,0:T(8,128)(2,1)}, bf16[8192,256]{1,0:T(8,128)(2,1)}, u32[]{:S(2)}, u32[]{:S(2)}) collective-permute-start(bf16[8192,256]{1,0:T(8,128)(2,1)} %all-gather.2.cloned.1.call-done), channel_id=1, source_target_pairs={{16,0},{32,16},{48,32},{64,48},{80,64},{96,80},{112,96},{128,112},... | collective-permute-start | bytes 12582920 | tf_op jit(solution)/shard_map/ppermute | solution.py:15
  61.7 103.1 %copy-start.2 = (s32[4]{0:T(128)S(1)}, s32[4]{0:T(128)}, u32[]{:S(2)}) copy-start(s32[4]{0:T(128)} %param.11) | copy-start | bytes 52
  181.9 8.7 %copy-start = (f32[5632,128,8]{1,0,2:T(8,128)}, f32[5632,128,8]{1,0,2:T(8,128)S(1)}, u32[]{:S(2)}) copy-start(f32[5632,128,8]{1,0,2:T(8,128)S(1)} %get-tuple-element.143) | copy-start | bytes 69206016 | tf_op jit(solution)/shard_map/while
  182.0 15.0 %copy-start.1 = (bf16[5632,256]{1,0:T(8,128)(2,1)S(1)}, bf16[5632,256]{1,0:T(8,128)(2,1)}, u32[]{:S(2)}) copy-start(bf16[5632,256]{1,0:T(8,128)(2,1)} %bitcast_select_fusion.2) | copy-start | bytes 8650756 | tf_op jit(solution)/shard_map/while
  226.2 8.7 %copy-start = (f32[5632,128,8]{1,0,2:T(8,128)}, f32[5632,128,8]{1,0,2:T(8,128)S(1)}, u32[]{:S(2)}) copy-start(f32[5632,128,8]{1,0,2:T(8,128)S(1)} %get-tuple-element.143) | copy-start | bytes 69206016 | tf_op jit(solution)/shard_map/while
  226.2 15.0 %copy-start.1 = (bf16[5632,256]{1,0:T(8,128)(2,1)S(1)}, bf16[5632,256]{1,0:T(8,128)(2,1)}, u32[]{:S(2)}) copy-start(bf16[5632,256]{1,0:T(8,128)(2,1)} %bitcast_select_fusion.2) | copy-start | bytes 8650756 | tf_op jit(solution)/shard_map/while
  270.4 8.7 %copy-start = (f32[5632,128,8]{1,0,2:T(8,128)}, f32[5632,128,8]{1,0,2:T(8,128)S(1)}, u32[]{:S(2)}) copy-start(f32[5632,128,8]{1,0,2:T(8,128)S(1)} %get-tuple-element.143) | copy-start | bytes 69206016 | tf_op jit(solution)/shard_map/while
  270.4 15.0 %copy-start.1 = (bf16[5632,256]{1,0:T(8,128)(2,1)S(1)}, bf16[5632,256]{1,0:T(8,128)(2,1)}, u32[]{:S(2)}) copy-start(bf16[5632,256]{1,0:T(8,128)(2,1)} %bitcast_select_fusion.2) | copy-start | bytes 8650756 | tf_op jit(solution)/shard_map/while
  314.7 8.7 %copy-start = (f32[5632,128,8]{1,0,2:T(8,128)}, f32[5632,128,8]{1,0,2:T(8,128)S(1)}, u32[]{:S(2)}) copy-start(f32[5632,128,8]{1,0,2:T(8,128)S(1)} %get-tuple-element.143) | copy-start | bytes 69206016 | tf_op jit(solution)/shard_map/while
  314.7 15.0 %copy-start.1 = (bf16[5632,256]{1,0:T(8,128)(2,1)S(1)}, bf16[5632,256]{1,0:T(8,128)(2,1)}, u32[]{:S(2)}) copy-start(bf16[5632,256]{1,0:T(8,128)(2,1)} %bitcast_select_fusion.2) | copy-start | bytes 8650756 | tf_op jit(solution)/shard_map/while
Sparse Core Ops, SparseCore 0:
  9.2 44.0 all-gather.1
where the time goes:
time: 350 us; the launch traced here: 349 us
  waiting for transfers between devices  133 us (38%)
  local copies, waits for them, and re-layouts  68.3 us (20%)
  matrix products  67.6 us (19%)
  other arithmetic  60.9 us (17%)
  between operations  13.4 us (4%)
  starting transfers between devices  5.21 us (1%)
    ppermute x2, waiting for transfers between devices, shifted(): return lax.ppermute(block, axis, route)  87.7 us
    all_gather x1, waiting for transfers between devices, body(): group_set = lax.all_gather(kv_shard, 'inner', axis=0, tiled=True)  45.1 us
    dot_general x4, matrix products, attend_block(): jnp.einsum('hqk,kd->hqd', rounded, value_rows, preferred_element_type=jnp...  44.9 us
    while x16, local copies, waits for them, and re-layouts  34.6 us
    reduce_sum x4, other arithmetic, attend_block(): total = jnp.sum(weights, axis=2, keepdims=True)  25.4 us
    dot_general x4, matrix products, attend_block(): jnp.einsum('qhd,kd->hqk', query_block, key_rows, preferred_element_type=j...  22.7 us
    gather x4, local copies, waits for them, and re-layouts, attend_block(): picked = jnp.take(window, block_list, axis=0).reshape(MAXB * BLOCK, 2 * HD)  21.2 us
    concatenate x1, other arithmetic, body(): window = jnp.concatenate([before_set, group_set, later_set], axis=0)  15.4 us
  transfers between devices with their start and end apart: 3, of which 2 were waited for; matrix products, arithmetic and copies ran while one was open for 1% of the time, Pallas kernels for 0%

commit v1 on v0

v1 whole, which is shorter than its diff:
```python
import functools

import jax
import jax.numpy as jnp
from jax import lax
from jax.experimental import pallas as pl
from jax.experimental.pallas import tpu as pltpu
from jax.sharding import PartitionSpec as P

HD = 128
HEADS = 8
BLOCK = 128
MAXB = 44
XS = 4
ZS = 8
CH = 4
GROUP_BLOCKS = 64
GROUPS = 16
SCALE = HD ** -0.5 * 1.4426950408889634
LIMIT = 2.0 ** 100
STEP = 2
MESH = pl.DeviceIdType.MESH

LINKS = ("xp", "xm", "y", "zp", "zm")
STEPS = (
    {"xp": (1, 0, 0), "xm": (3, 0, 0), "y": (0, 1, 0), "zp": (0, 0, 1), "zm": (0, 0, -1)},
    {"xp": (2, 0, 0), "xm": (3, 1, 0), "y": (1, 1, 0), "zp": (1, 0, 1), "zm": (3, 0, -1)},
    {"xp": (2, 0, 1), "xm": (2, 0, -1), "y": (2, 1, 0), "zp": (0, 1, 1), "zm": (0, 1, -1)},
    {"xp": (1, 1, 1), "xm": (3, 1, -1), "y": (2, 1, 1), "zp": (3, 0, 1), "zm": (1, 0, -1)},
)
LAST = (
    (("xp", (1, 1, -1), 0), ("xm", (3, 1, 1), 0), ("y", (2, 1, -1), 0), ("zp", (3, 1, 1), 2), ("zm", (1, 1, -1), 2)),
    (("xp", (1, 1, -1), 1), ("xm", (3, 1, 1), 1), ("y", (2, 1, -1), 1), ("zp", (3, 1, 1), 3), ("zm", (1, 1, -1), 3)),
    (("xm", (2, 1, -1), 2), ("y", (2, 1, -1), 3)),
)


def gather_kernel(k_ref, v_ref, win, own_sem, send_sem, recv_sem, sib_send, sib_recv):
    g = lax.axis_index("outer")
    inner = lax.axis_index("inner")
    core = inner % 2
    x = inner // 2 % XS
    y = inner // (2 * XS)
    cross_up = jnp.where(g % ZS == ZS - 1, 1, 0)
    cross_down = jnp.where(g % ZS == 0, 1, 0)
    up, down = (g + 1) % GROUPS, (g + GROUPS - 1) % GROUPS

    def place(px, py):
        return (py * XS + px) * 2 + core

    target = {
        "xp": (g, place((x + XS - 1) % XS, y)),
        "xm": (g, place((x + 1) % XS, y)),
        "y": (g, place(x, 1 - y)),
        "zp": (down, place(x, (y + cross_down) % 2)),
        "zm": (up, place(x, (y + cross_up) % 2)),
    }
    sibling = (g, (y * XS + x) * 2 + 1 - core)

    def slot(piece):
        dx, dy, dz = piece
        turn = {0: 0, 1: cross_up, -1: cross_down}[dz]
        return dz + 1, place((x + dx) % XS, (y + dy + turn) % 2)

    def sent(link, piece):
        dx, dy, dz = piece
        by = {
            "xp": ((dx + XS - 1) % XS, dy, dz),
            "xm": ((dx + 1) % XS, dy, dz),
            "y": (dx, 1 - dy, dz),
            "zp": (dx, dy, dz - 1),
            "zm": (dx, dy, dz + 1),
        }[link]
        return by, dz + 1

    def link_copy(link, piece, c, step):
        n = LINKS.index(link)
        mine, there = sent(link, piece)
        a, b = slot(mine)
        return pltpu.make_async_remote_copy(
            src_ref=win.at[a, b, c],
            dst_ref=win.at[there, b, c],
            send_sem=send_sem.at[n, step, c],
            recv_sem=recv_sem.at[n, step, c],
            device_id=target[link],
            device_id_type=MESH,
        )

    def arrival(link, piece, c, step):
        n = LINKS.index(link)
        a, b = slot(piece)
        return pltpu.make_async_remote_copy(
            src_ref=win.at[a, b, c],
            dst_ref=win.at[a, b, c],
            send_sem=send_sem.at[n, step, c],
            recv_sem=recv_sem.at[n, step, c],
            device_id=target[link],
            device_id_type=MESH,
        )

    def sib_copy(piece, c, n, step):
        a, b = slot(piece)
        return pltpu.make_async_remote_copy(
            src_ref=win.at[a, b, c],
            dst_ref=win.at[a, b, c],
            send_sem=sib_send.at[n, step, c],
            recv_sem=sib_recv.at[n, step, c],
            device_id=sibling,
            device_id_type=MESH,
        )

    def sib_arrival(piece, c, n, step):
        a, b = slot(piece)
        return pltpu.make_async_remote_copy(
            src_ref=win.at[a, b, c],
            dst_ref=win.at[a, b + 1 - 2 * core, c],
            send_sem=sib_send.at[n, step, c],
            recv_sem=sib_recv.at[n, step, c],
            device_id=sibling,
            device_id_type=MESH,
        )

    own = (0, 0, 0)
    _, here = slot(own)
    fill = []
    for c in range(CH):
        rows = pl.ds(c * BLOCK, BLOCK)
        for part, ref in enumerate((k_ref, v_ref)):
            copy = pltpu.make_async_copy(ref.at[rows], win.at[1, here, c, part], own_sem.at[c, part])
            copy.start()
            fill.append(copy)

    barrier = pltpu.get_barrier_semaphore()
    for device in (*target.values(), sibling):
        pl.semaphore_signal(barrier, inc=1, device_id=device, device_id_type=MESH)
    pl.semaphore_wait(barrier, len(target) + 1)

    def tick(step, c):
        if step > 0:
            for n, link in enumerate(LINKS):
                piece = STEPS[step - 1][link]
                arrival(link, piece, c, step - 1).wait_recv()
        for n, link in enumerate(LINKS):
            link_copy(link, STEPS[step][link], c, step).start()
        if step > 0:
            for n, link in enumerate(LINKS):
                sib_copy(STEPS[step - 1][link], c, n, step - 1).start()
        else:
            sib_copy(own, c, len(LINKS), 0).start()

    for c in range(CH):
        fill[2 * c].wait()
        fill[2 * c + 1].wait()
        tick(0, c)
    for step in range(1, len(STEPS)):
        lax.fori_loop(0, CH, lambda c, _, step=step: (tick(step, c), 0)[1], 0)

    last = len(STEPS)
    for i in range(CH):
        for n, link in enumerate(LINKS):
            arrival(link, STEPS[last - 1][link], i, last - 1).wait_recv()
        if i < len(LAST):
            for link, piece, c in LAST[i]:
                link_copy(link, piece, c, last).start()
        for n, link in enumerate(LINKS):
            sib_copy(STEPS[last - 1][link], i, n, last - 1).start()
    for row in LAST:
        for link, piece, c in row:
            arrival(link, piece, c, last).wait_recv()
            sib_copy(piece, c, LINKS.index(link), last).start()

    def drain(c, _):
        for step in range(len(STEPS)):
            for n, link in enumerate(LINKS):
                piece = STEPS[step][link]
                link_copy(link, piece, c, step).wait_send()
                sib_copy(piece, c, n, step).wait_send()
                sib_arrival(piece, c, n, step).wait_recv()
        sib_copy(own, c, len(LINKS), 0).wait_send()
        sib_arrival(own, c, len(LINKS), 0).wait_recv()
        return 0

    lax.fori_loop(0, CH, drain, 0)
    for row in LAST:
        for link, piece, c in row:
            n = LINKS.index(link)
            link_copy(link, piece, c, last).wait_send()
            sib_copy(piece, c, n, last).wait_send()
            sib_arrival(piece, c, n, last).wait_recv()


def gather(keys, values):
    steps = len(STEPS) + 1
    return pl.pallas_call(
        gather_kernel,
        out_shape=jax.ShapeDtypeStruct((3, GROUP_BLOCKS // CH, CH, 2, BLOCK, HD), jnp.bfloat16),
        in_specs=[pl.BlockSpec(memory_space=pl.ANY)] * 2,
        out_specs=pl.BlockSpec(memory_space=pl.ANY),
        scratch_shapes=[
            pltpu.SemaphoreType.DMA((CH, 2)),
            pltpu.SemaphoreType.DMA((len(LINKS), steps, CH)),
            pltpu.SemaphoreType.DMA((len(LINKS), steps, CH)),
            pltpu.SemaphoreType.DMA((len(LINKS) + 1, steps, CH)),
            pltpu.SemaphoreType.DMA((len(LINKS) + 1, steps, CH)),
        ],
        compiler_params=pltpu.CompilerParams(collective_id=0, has_side_effects=True),
    )(keys, values)


def nt_dot(a, b):
    return lax.dot_general(a, b, (((1,), (1,)), ((), ())), preferred_element_type=jnp.float32)


def attend_kernel(blocks, counts, q_ref, win, o_ref, kv, shift, acc, sem):
    i = pl.program_id(0)
    g = lax.axis_index("outer")
    half = i % 2

    def fetch(row, side, e):
        block = blocks[row, e]
        group = (block // GROUP_BLOCKS - g + 1 + GROUPS) % GROUPS
        return pltpu.make_async_copy(
            win.at[group * GROUP_BLOCKS + block % GROUP_BLOCKS], kv.at[side, e], sem.at[side, e]
        )

    def entries(row):
        return (counts[row] + STEP - 1) // STEP * STEP

    def fetch_row(row, side):
        lax.fori_loop(0, entries(row), lambda e, _: (fetch(row, side, e).start(), 0)[1], 0)

    @pl.when(i == 0)
    def _():
        fetch_row(0, 0)

    @pl.when(i + 1 < pl.num_programs(0))
    def _():
        fetch_row(i + 1, 1 - half)

    count = counts[i]
    queries = [q_ref[:, h * HD:(h + 1) * HD] for h in range(HEADS)]
    acc[...] = jnp.zeros_like(acc)

    def attend(s, _):
        first = s * STEP
        for e in range(STEP):
            fetch(i, half, first + e).wait()

        @pl.when(s == 0)
        def _():
            k = kv[half, 0, 0]
            for h in range(HEADS):
                peak = jnp.max(nt_dot(q_ref[:, h * HD:(h + 1) * HD], k), axis=1, keepdims=True)
                shift[h] = jnp.broadcast_to(peak * SCALE, (BLOCK, HD))

        k = jnp.concatenate([kv[half, first + e, 0] for e in range(STEP)], axis=0)
        v = []
        for e in range(STEP):
            live = jnp.where(first + e < count, 1.0, 0.0).astype(jnp.float32)
            ones = jnp.full((BLOCK, HD), live, jnp.float32).astype(jnp.bfloat16)
            v.append(jnp.concatenate([kv[half, first + e, 1] * ones, ones], axis=1))
        v = jnp.concatenate(v, axis=0)
        for h in range(HEADS):
            scores = nt_dot(q_ref[:, h * HD:(h + 1) * HD], k)
            m = jnp.concatenate([shift[h]] * STEP, axis=1)
            weights = jnp.exp2(scores * SCALE - m).astype(jnp.bfloat16)
            acc[h] += jnp.dot(weights, v, preferred_element_type=jnp.float32)
        return 0

    lax.fori_loop(0, entries(i) // STEP, attend, 0)
    top = jnp.max(acc[:, :, HD:])
    safe = top < LIMIT

    @pl.when(jnp.logical_not(safe))
    def _():
        def head(h, _):
            q = jnp.zeros((BLOCK, HD), jnp.bfloat16)
            for n in range(HEADS):
                q = jnp.where(h == n, queries[n], q)

            def one(e, state):
                peak, total, mixed = state
                scores = nt_dot(q, kv[half, e, 0]) * SCALE
                new = jnp.maximum(peak, jnp.max(scores, axis=1, keepdims=True))
                weights = jnp.exp2(scores - new)
                keep = jnp.exp2(peak - new)
                total = total * keep + jnp.sum(weights, axis=1, keepdims=True)
                mixed = mixed * keep + jnp.dot(
                    weights.astype(jnp.bfloat16), kv[half, e, 1], preferred_element_type=jnp.float32
                )
                return new, total, mixed

            start = (
                jnp.full((BLOCK, 1), -1e30, jnp.float32),
                jnp.zeros((BLOCK, 1), jnp.float32),
                jnp.zeros((BLOCK, HD), jnp.float32),
            )
            _, total, mixed = lax.fori_loop(0, count, one, start)
            acc[h] = jnp.concatenate([mixed, jnp.broadcast_to(total, (BLOCK, HD))], axis=1)
            return 0

        lax.fori_loop(0, HEADS, head, 0)

    for h in range(HEADS):
        o_ref[:, h * HD:(h + 1) * HD] = (acc[h, :, :HD] / acc[h, :, HD:]).astype(jnp.bfloat16)


def attend(blocks, counts, queries, window):
    rows = queries.shape[0] // BLOCK
    return pl.pallas_call(
        attend_kernel,
        grid_spec=pltpu.PrefetchScalarGridSpec(
            num_scalar_prefetch=2,
            grid=(rows,),
            in_specs=[
                pl.BlockSpec((BLOCK, HEADS * HD), lambda i, *_: (i, 0)),
                pl.BlockSpec(memory_space=pl.ANY),
            ],
            out_specs=pl.BlockSpec((BLOCK, HEADS * HD), lambda i, *_: (i, 0)),
            scratch_shapes=[
                pltpu.VMEM((2, MAXB, 2, BLOCK, HD), jnp.bfloat16),
                pltpu.VMEM((HEADS, BLOCK, HD), jnp.float32),
                pltpu.VMEM((HEADS, BLOCK, 2 * HD), jnp.float32),
                pltpu.SemaphoreType.DMA((2, MAXB)),
            ],
        ),
        out_shape=jax.ShapeDtypeStruct(queries.shape, jnp.bfloat16),
        compiler_params=pltpu.CompilerParams(vmem_limit_bytes=32 * 2 ** 20),
    )(blocks, counts, queries, window)


def body(queries, keys, values, key_blocks, key_counts):
    window = gather(keys, values)
    window = window.reshape(3 * GROUP_BLOCKS, 2, BLOCK, HD)
    return attend(key_blocks, key_counts, queries, window)


def solution(mesh):
    placed = (
        P(("outer", "inner"), None),
        P(("outer", "inner"), None),
        P(("outer", "inner"), None),
        P(("outer", "inner"), None),
        P(("outer", "inner")),
    )
    return jax.shard_map(
        body, mesh=mesh, in_specs=placed, out_specs=P(("outer", "inner"), None), check_vma=False
    )
```

time: 350 us -> 103 us (0.29)
  the two profiles are of different devices: /device:TPU:1 before, /device:TPU:73 now
where the time goes in v1:
time: 103 us
  Pallas kernels  98.7 us (96%)
  local copies, waits for them, and re-layouts  4.58 us (4%)
    pallas_call x1, Pallas kernels, attend(): pl.pallas_call(attend_kernel, grid_spec=pltpu.PrefetchScalarGridSpec(num_...  57.3 us
    pallas_call x1, Pallas kernels, gather(): pl.pallas_call(gather_kernel, out_shape=jax.ShapeDtypeStruct((3, GROUP_BL...  41.5 us
    unnamed x8, local copies, waits for them, and re-layouts  4.58 us

profile of v1, /device:TPU:73, one launch (start us, length us, event | category | flops | bytes accessed | tf_op | source)
XLA Modules:
  0.0 103.4 jit_solution(1851945133301929585)
XLA Ops:
  0.0 0.0 copy-start.3
  0.0 0.0 copy-start.2
  0.0 0.0 copy-start.1
  0.0 41.5 %shard_map.55 = bf16[3,16,4,2,128,128]{5,4,3,2,1,0:T(8,128)(2,1)} custom-call(bf16[512,128]{1,0:T(8,128)(2,1)} %k_ref.1, bf16[512,128]{1,0:T(8,128)(2,1)} %v_ref.1), custom_call_target="tpu_custom_call" | custom-call | tf_op jit(solution)/shard_map/pallas_call | solution.py:194
  41.5 0.0 copy-done.3
  41.5 0.0 copy-done.2
  41.5 0.0 copy-done.1
  41.5 0.0 copy-start
  41.5 4.6 %copy-done = bf16[3,16,4,2,128,128]{5,4,3,2,1,0:T(8,128)(2,1)S(1)} copy-done((bf16[3,16,4,2,128,128]{5,4,3,2,1,0:T(8,128)(2,1)S(1)}, bf16[3,16,4,2,128,128]{5,4,3,2,1,0:T(8,128)(2,1)}, u32[]{:S(2)}) %copy-start) | copy-done | bytes 12582936
  46.1 57.3 %shard_map.56 = bf16[512,1024]{1,0:T(8,128)(2,1)} custom-call(s32[4,44]{1,0:T(4,128)S(1)} %copy-done.2, s32[4]{0:T(128)S(1)} %copy-done.3, bf16[512,1024]{1,0:T(8,128)(2,1)S(1)} %copy-done.1, bf16[192,2,128,128]{3,2,1,0:T(8,128)(2,1)S(1)} %bitcast.1), custom_call_target="tpu_custom_call" | custom-call | tf_op jit(solution)/shard_map/pallas_call | solution.py:310
Async XLA Ops:
  0.0 41.5 %copy-start.3 = (s32[4]{0:T(128)S(1)}, s32[4]{0:T(128)}, u32[]{:S(2)}) copy-start(s32[4]{0:T(128)} %counts.1) | copy-start | bytes 52
  0.0 41.5 %copy-start.2 = (s32[4,44]{1,0:T(4,128)S(1)}, s32[4,44]{1,0:T(4,128)}, u32[]{:S(2)}) copy-start(s32[4,44]{1,0:T(4,128)} %blocks.1) | copy-start | bytes 2116
  0.0 41.5 %copy-start.1 = (bf16[512,1024]{1,0:T(8,128)(2,1)S(1)}, bf16[512,1024]{1,0:T(8,128)(2,1)}, u32[]{:S(2)}) copy-start(bf16[512,1024]{1,0:T(8,128)(2,1)} %q_ref.1) | copy-start | bytes 3145732
  41.5 4.6 %copy-start = (bf16[3,16,4,2,128,128]{5,4,3,2,1,0:T(8,128)(2,1)S(1)}, bf16[3,16,4,2,128,128]{5,4,3,2,1,0:T(8,128)(2,1)}, u32[]{:S(2)}) copy-start(bf16[3,16,4,2,128,128]{5,4,3,2,1,0:T(8,128)(2,1)} %shard_map.55) | copy-start | bytes 37748740

commit v2 on v0

v2 whole, which is shorter than its diff:
```python
import functools

import jax
import jax.numpy as jnp
from jax import lax
from jax.experimental import pallas as pl
from jax.experimental.pallas import tpu as pltpu
from jax.sharding import PartitionSpec as P

HD = 128
HEADS = 8
BLOCK = 128
MAXB = 44
XS = 4
ZS = 8
CH = 4
GROUP_BLOCKS = 64
STEP = 4
TILE = 2 * HD
GROUPS = 16
SCALE = HD ** -0.5 * 1.4426950408889634
LIMIT = 2.0 ** 100
DEAD = 1e30
MESH = pl.DeviceIdType.MESH

LINKS = ("xp", "xm", "y", "zp", "zm")
STEPS = (
    {"xp": (1, 0, 0), "xm": (3, 0, 0), "y": (0, 1, 0), "zp": (0, 0, 1), "zm": (0, 0, -1)},
    {"xp": (2, 0, 0), "xm": (3, 0, 1), "y": (1, 1, 0), "zp": (1, 0, 1), "zm": (3, 0, -1)},
    {"xp": (1, 0, -1), "xm": (3, 1, 0), "y": (2, 1, 0), "zp": (0, 1, 1), "zm": (0, 1, -1)},
    {"xp": (2, 0, 1), "xm": (2, 0, -1), "y": (3, 1, 1), "zp": (1, 1, 1), "zm": (1, 1, -1)},
)
LAST = (
    (("xm", (3, 1, -1), 0), ("y", (3, 1, -1), 2), ("zp", (2, 1, 1), 1), ("zm", (2, 1, -1), 1)),
    (("xp", (2, 1, 1), 0), ("xm", (3, 1, -1), 1), ("y", (3, 1, -1), 3), ("zp", (2, 1, 1), 2), ("zm", (2, 1, -1), 2)),
    (("y", (2, 1, -1), 0), ("zp", (2, 1, 1), 3), ("zm", (2, 1, -1), 3)),
)
ORDER = ((0, 0, 0),) + tuple(row[link] for row in STEPS for link in LINKS) + ((3, 1, -1), (2, 1, 1), (2, 1, -1))
TICKS = CH * len(STEPS) + len(LAST)
AHEAD = 4


def parent(link, piece):
    dx, dy, dz = piece
    return {
        "xp": ((dx + XS - 1) % XS, dy, dz),
        "xm": ((dx + 1) % XS, dy, dz),
        "y": (dx, 1 - dy, dz),
        "zp": (dx, dy, dz - 1),
        "zm": (dx, dy, dz + 1),
    }[link]


def position():
    g = lax.axis_index("outer")
    inner = lax.axis_index("inner")
    cross_up = jnp.where(g % ZS == ZS - 1, 1, 0)
    cross_down = jnp.where(g % ZS == 0, 1, 0)
    return g, inner // (2 * XS), inner // 2 % XS, inner % 2, cross_up, cross_down


def gather_kernel(k_ref, v_ref, win, stage, own_sem, send_sem, recv_sem, sib_send, sib_recv):
    g, y, x, core, cross_up, cross_down = position()
    up, down = (g + 1) % GROUPS, (g + GROUPS - 1) % GROUPS

    def place(px, py):
        return (py * XS + px) * 2 + core

    target = {
        "xp": (g, place((x + XS - 1) % XS, y)),
        "xm": (g, place((x + 1) % XS, y)),
        "y": (g, place(x, 1 - y)),
        "zp": (down, place(x, (y + cross_down) % 2)),
        "zm": (up, place(x, (y + cross_up) % 2)),
    }
    sibling = (g, (y * XS + x) * 2 + 1 - core)

    def at(piece, c):
        return win.at[ORDER.index(piece), core, c]

    def source(piece, c):
        return stage.at[c] if piece == ORDER[0] else at(piece, c)

    def link_copy(link, piece, c, t):
        n = LINKS.index(link)
        return pltpu.make_async_remote_copy(
            src_ref=source(parent(link, piece), c),
            dst_ref=at(piece, c),
            send_sem=send_sem.at[n, t],
            recv_sem=recv_sem.at[n, t],
            device_id=target[link],
            device_id_type=MESH,
        )

    def sib_copy(piece, c, n, t):
        return pltpu.make_async_remote_copy(
            src_ref=source(piece, c),
            dst_ref=at(piece, c),
            send_sem=sib_send.at[n, t],
            recv_sem=sib_recv.at[n, t],
            device_id=sibling,
            device_id_type=MESH,
        )

    def sib_arrival(piece, c, n, t):
        here = win.at[ORDER.index(piece), 1 - core, c]
        return pltpu.make_async_remote_copy(
            src_ref=here,
            dst_ref=here,
            send_sem=sib_send.at[n, t],
            recv_sem=sib_recv.at[n, t],
            device_id=sibling,
            device_id_type=MESH,
        )

    barrier = pltpu.get_barrier_semaphore()
    for device in (*target.values(), sibling):
        pl.semaphore_signal(barrier, inc=1, device_id=device, device_id_type=MESH)
    fill = []
    for c in range(CH):
        rows = pl.ds(c * BLOCK, BLOCK)
        stage[c, 0] = k_ref[rows]
        stage[c, 1] = v_ref[rows].T
        copy = pltpu.make_async_copy(stage.at[c], at(ORDER[0], c), own_sem.at[c])
        copy.start()
        fill.append(copy)
    pl.semaphore_wait(barrier, len(target) + 1)

    def row(step, c):
        if step < len(STEPS):
            return [(link, STEPS[step][link], c) for link in LINKS]
        return LAST[c]

    def tick(step, c):
        t = step * CH + c
        if isinstance(t, int) and t < CH:
            arrived = ()
        else:
            arrived = row(step - 1, c)
        for link, piece, chunk in arrived:
            link_copy(link, piece, chunk, t - CH).wait_recv()
        for link, piece, chunk in row(step, c) if not (step == len(STEPS) and c >= len(LAST)) else ():
            if not (isinstance(t, int) and t < AHEAD):
                link_copy(link, piece, chunk, t - AHEAD).wait_send()
            link_copy(link, piece, chunk, t).start()
        for link, piece, chunk in arrived:
            sib_copy(piece, chunk, LINKS.index(link), t - CH).start()
        if step == 0:
            sib_copy(ORDER[0], c, len(LINKS), t).start()

    for c in range(CH):
        tick(0, c)
    for step in range(1, len(STEPS)):
        lax.fori_loop(0, CH, lambda c, _, step=step: (tick(step, c), 0)[1], 0)
    for c in range(CH):
        tick(len(STEPS), c)
    for c, last in enumerate(LAST):
        t = TICKS - len(LAST) + c
        for link, piece, chunk in last:
            link_copy(link, piece, chunk, t).wait_recv()
            sib_copy(piece, chunk, LINKS.index(link), t).start()

    sent = {link: [] for link in LINKS}
    for t in range(TICKS):
        for link, piece, chunk in row(t // CH, t % CH):
            if t >= AHEAD:
                sent[link].remove(t - AHEAD)
            sent[link].append(t)
    for link in LINKS:
        for t in sent[link]:
            link_copy(link, ORDER[1], 0, t).wait_send()
    for copy in fill:
        copy.wait()

    def drain(c, _):
        for step in range(len(STEPS)):
            for link, piece, chunk in row(step, c):
                sib_copy(piece, chunk, LINKS.index(link), step * CH + c).wait_send()
                sib_arrival(piece, chunk, LINKS.index(link), step * CH + c).wait_recv()
        sib_copy(ORDER[0], c, len(LINKS), c).wait_send()
        sib_arrival(ORDER[0], c, len(LINKS), c).wait_recv()
        return 0

    lax.fori_loop(0, CH, drain, 0)
    for c, last in enumerate(LAST):
        for link, piece, chunk in last:
            t = TICKS - len(LAST) + c
            sib_copy(piece, chunk, LINKS.index(link), t).wait_send()
            sib_arrival(piece, chunk, LINKS.index(link), t).wait_recv()


def gather(keys, values):
    return pl.pallas_call(
        gather_kernel,
        out_shape=jax.ShapeDtypeStruct((len(ORDER), 2, CH, 2, BLOCK, HD), jnp.bfloat16),
        in_specs=[pl.BlockSpec(memory_space=pltpu.VMEM)] * 2,
        out_specs=pl.BlockSpec(memory_space=pl.ANY),
        scratch_shapes=[
            pltpu.VMEM((CH, 2, BLOCK, HD), jnp.bfloat16),
            pltpu.SemaphoreType.DMA((CH,)),
            pltpu.SemaphoreType.DMA((len(LINKS), TICKS)),
            pltpu.SemaphoreType.DMA((len(LINKS), TICKS)),
            pltpu.SemaphoreType.DMA((len(LINKS) + 1, TICKS)),
            pltpu.SemaphoreType.DMA((len(LINKS) + 1, TICKS)),
        ],
        compiler_params=pltpu.CompilerParams(collective_id=0, has_side_effects=True),
    )(keys, values)


def nt_dot(a, b):
    return lax.dot_general(a, b, (((1,), (1,)), ((), ())), preferred_element_type=jnp.float32)


def query_tile(q_ref, row, t):
    rows = pl.ds(pl.multiple_of(row * BLOCK, BLOCK), BLOCK)
    return jnp.concatenate([q_ref[rows, h * HD:(h + 1) * HD] for h in (2 * t, 2 * t + 1)], axis=0)


def attend_kernel(
    blocks, counts, q_ref, k_ref, win, o_ref, kv, scores, shift, total, acc, places, rows_of, live, first_of, sem
):
    g, y, x, _, cross_up, cross_down = position()
    lists = q_ref.shape[0] // BLOCK
    tiles = [pl.ds(t * TILE, TILE) for t in range(HEADS * HD // TILE)]

    for i, (dx, dy, dz) in enumerate(ORDER):
        places[(dz + 1) * 2 * XS + dy * XS + dx] = i

    def rank(block):
        group = (block // GROUP_BLOCKS - g + 1 + GROUPS) % GROUPS
        device = block % GROUP_BLOCKS // CH
        turn = jnp.where(group == 2, cross_up, jnp.where(group == 0, cross_down, 0))
        dx = (device // 2 % XS - x + XS) % XS
        dy = (device // (2 * XS) + y + turn) % 2
        return (places[group * 2 * XS + dy * XS + dx] * 2 + device % 2) * CH + block % CH

    def fetch(n, e, source):
        return pltpu.make_async_copy(win.at[source], kv.at[n, e], sem.at[n, e])

    def plan(row, n):
        count = counts[row]
        first_of[row] = n

        def one(s, n):
            rows_of[n] = row
            for e in range(STEP):
                live[n, e] = (s * STEP + e < count).astype(jnp.int32)
                fetch(n, e, rank(blocks[row, s * STEP + e])).start()
            return n + 1

        return lax.fori_loop(0, (count + STEP - 1) // STEP, one, n)

    steps = lax.fori_loop(0, lists, plan, 0)

    def wait(n):
        for e in range(STEP):
            fetch(n, e, 0).wait()

    total[...] = jnp.zeros_like(total)
    acc[...] = jnp.zeros_like(acc)

    def peaks(row, _):
        own = k_ref[pl.ds(pl.multiple_of(row * BLOCK, BLOCK), BLOCK)]
        for t, c in enumerate(tiles):
            s = nt_dot(own, query_tile(q_ref, row, t))
            shift[row, :, c] = jnp.broadcast_to(jnp.max(s, axis=0, keepdims=True) * SCALE, (8, TILE))
        return 0

    lax.fori_loop(0, lists, peaks, 0)

    def keys_of(n):
        return jnp.concatenate([kv[n, e, 0] for e in range(STEP)], axis=0)

    wait(0)
    for t, c in enumerate(tiles):
        scores[:, c] = nt_dot(keys_of(0), query_tile(q_ref, 0, t))

    def step(n, _):
        row = rows_of[n]
        following = jnp.minimum(n + 1, steps - 1)

        @pl.when(n + 1 < steps)
        def _():
            wait(n + 1)

        next_row = rows_of[following]
        k = keys_of(following)
        v = jnp.concatenate([kv[n, e, 1] for e in range(STEP)], axis=1)
        for t, c in enumerate(tiles):
            base = shift[row, 0:1, c]
            parts = []
            for e in range(STEP):
                m = jnp.where(live[n, e] == 1, base, DEAD)
                parts.append(jnp.exp2(scores[pl.ds(e * BLOCK, BLOCK), c] * SCALE - m))
            scores[:, c] = nt_dot(k, query_tile(q_ref, next_row, t))
            weights = jnp.concatenate(parts, axis=0)
            total[row, :, c] += jnp.sum(weights.reshape(STEP * BLOCK // 8, 8, TILE), axis=0)
            acc[row, :, c] += jnp.dot(v, weights.astype(jnp.bfloat16), preferred_element_type=jnp.float32)
        return 0

    lax.fori_loop(0, steps, step, 0)

    def finish(row, _):
        sums = jnp.sum(total[row], axis=0, keepdims=True)
        safe = jnp.max(sums) < LIMIT

        @pl.when(jnp.logical_not(safe))
        def _():
            for t, c in enumerate(tiles):
                q = query_tile(q_ref, row, t)

                def one(e, state, q=q):
                    peak, tot, mixed = state
                    n = first_of[row] + e // STEP
                    s = nt_dot(kv[n, e % STEP, 0], q) * SCALE
                    new = jnp.maximum(peak, jnp.max(s, axis=0, keepdims=True))
                    weights = jnp.exp2(s - new)
                    keep = jnp.exp2(peak - new)
                    tot = tot * keep + jnp.sum(weights, axis=0, keepdims=True)
                    mixed = mixed * keep + jnp.dot(
                        kv[n, e % STEP, 1], weights.astype(jnp.bfloat16), preferred_element_type=jnp.float32
                    )
                    return new, tot, mixed

                start = (
                    jnp.full((1, TILE), -DEAD, jnp.float32),
                    jnp.zeros((1, TILE), jnp.float32),
                    jnp.zeros((HD, TILE), jnp.float32),
                )
                _, tot, mixed = lax.fori_loop(0, counts[row], one, start)
                total[row, :, c] = jnp.concatenate([tot, jnp.zeros((7, TILE), jnp.float32)], axis=0)
                acc[row, :, c] = mixed

        sums = jnp.sum(total[row], axis=0, keepdims=True)
        rows = pl.ds(pl.multiple_of(row * BLOCK, BLOCK), BLOCK)
        for h in range(HEADS):
            c = slice(h * HD, (h + 1) * HD)
            o_ref[rows, c] = (acc[row, :, c] / sums[:, c]).T.astype(jnp.bfloat16)
        return 0

    lax.fori_loop(0, lists, finish, 0)


def attend(blocks, counts, queries, keys, window):
    lists = queries.shape[0] // BLOCK
    steps = lists * (MAXB // STEP)
    rows = HEADS * BLOCK
    return pl.pallas_call(
        attend_kernel,
        in_specs=[pl.BlockSpec(memory_space=pltpu.SMEM)] * 2
        + [pl.BlockSpec(memory_space=pltpu.VMEM)] * 2
        + [pl.BlockSpec(memory_space=pl.ANY)],
        out_specs=pl.BlockSpec(memory_space=pltpu.VMEM),
        scratch_shapes=[
            pltpu.VMEM((steps, STEP, 2, BLOCK, HD), jnp.bfloat16),
            pltpu.VMEM((STEP * BLOCK, rows), jnp.float32),
            pltpu.VMEM((lists, 8, rows), jnp.float32),
            pltpu.VMEM((lists, 8, rows), jnp.float32),
            pltpu.VMEM((lists, HD, rows), jnp.float32),
            pltpu.SMEM((len(ORDER),), jnp.int32),
            pltpu.SMEM((steps,), jnp.int32),
            pltpu.SMEM((steps, STEP), jnp.int32),
            pltpu.SMEM((lists,), jnp.int32),
            pltpu.SemaphoreType.DMA((steps, STEP)),
        ],
        out_shape=jax.ShapeDtypeStruct(queries.shape, jnp.bfloat16),
        compiler_params=pltpu.CompilerParams(vmem_limit_bytes=40 * 2 ** 20),
    )(blocks, counts, queries, keys, window)


def body(queries, keys, values, key_blocks, key_counts):
    window = gather(keys, values)
    window = window.reshape(len(ORDER) * 2 * CH, 2, BLOCK, HD)
    return attend(key_blocks, key_counts, queries, keys, window)


def solution(mesh):
    placed = (
        P(("outer", "inner"), None),
        P(("outer", "inner"), None),
        P(("outer", "inner"), None),
        P(("outer", "inner"), None),
        P(("outer", "inner")),
    )
    return jax.shard_map(
        body, mesh=mesh, in_specs=placed, out_specs=P(("outer", "inner"), None), check_vma=False
    )
```

time: 350 us -> 91.3 us (0.26)
  the two profiles are of different devices: /device:TPU:1 before, /device:TPU:2 now
where the time goes in v2:
time: 91.3 us; the launch traced here: 91.1 us
  Pallas kernels  86.5 us (95%)
  local copies, waits for them, and re-layouts  4.58 us (5%)
    pallas_call x1, Pallas kernels, gather(): pl.pallas_call(gather_kernel, out_shape=jax.ShapeDtypeStruct((len(ORDER),...  45.9 us
    pallas_call x1, Pallas kernels, attend(): pl.pallas_call(attend_kernel, in_specs=[pl.BlockSpec(memory_space=pltpu.S...  40.6 us
    unnamed x10, local copies, waits for them, and re-layouts  4.58 us

profile of v2, /device:TPU:2, one launch (start us, length us, event | category | flops | bytes accessed | tf_op | source)
XLA Modules:
  0.0 91.1 jit_solution(4122087556684275746)
XLA Ops:
  0.0 0.0 copy-start.2
  0.0 0.0 copy-start.4
  0.0 0.0 copy-start.3
  0.0 0.0 copy-start.1
  0.0 45.9 %shard_map.55 = bf16[24,2,4,2,128,128]{5,4,3,2,1,0:T(8,128)(2,1)} custom-call(bf16[512,128]{1,0:T(8,128)(2,1)} %k_ref.3, bf16[512,128]{1,0:T(8,128)(2,1)} %v_ref.1), custom_call_target="tpu_custom_call" | custom-call | tf_op jit(solution)/shard_map/pallas_call | solution.py:193
  45.9 0.0 copy-done.2
  45.9 0.0 copy-done.4
  45.9 0.0 copy-done.3
  45.9 0.0 copy-done.1
  45.9 0.0 copy-start
  45.9 4.6 %copy-done = bf16[24,2,4,2,128,128]{5,4,3,2,1,0:T(8,128)(2,1)S(1)} copy-done((bf16[24,2,4,2,128,128]{5,4,3,2,1,0:T(8,128)(2,1)S(1)}, bf16[24,2,4,2,128,128]{5,4,3,2,1,0:T(8,128)(2,1)}, u32[]{:S(2)}) %copy-start) | copy-done | bytes 12582936
  50.5 40.6 %shard_map.56 = bf16[512,1024]{1,0:T(8,128)(2,1)} custom-call(s32[4,44]{1,0:T(4,128)S(1)} %copy-done.3, s32[4]{0:T(128)S(1)} %copy-done.4, bf16[512,1024]{1,0:T(8,128)(2,1)S(1)} %copy-done.1, bf16[512,128]{1,0:T(8,128)(2,1)S(1)} %copy-done.2, bf16[192,2,128,128]{3,2,1,0:T(8,128)(2,1)S(1)} %bitcast.1), custom_call_target="tpu_custom_call" | custom-call | tf_op jit(solution)/shard_map/pallas_call | solution.py:348
Async XLA Ops:
  0.0 45.9 %copy-start.2 = (bf16[512,128]{1,0:T(8,128)(2,1)S(1)}, bf16[512,128]{1,0:T(8,128)(2,1)}, u32[]{:S(2)}) copy-start(bf16[512,128]{1,0:T(8,128)(2,1)} %k_ref.3) | copy-start | bytes 393220
  0.0 45.9 %copy-start.4 = (s32[4]{0:T(128)S(1)}, s32[4]{0:T(128)}, u32[]{:S(2)}) copy-start(s32[4]{0:T(128)} %counts.1) | copy-start | bytes 52
  0.0 45.9 %copy-start.3 = (s32[4,44]{1,0:T(4,128)S(1)}, s32[4,44]{1,0:T(4,128)}, u32[]{:S(2)}) copy-start(s32[4,44]{1,0:T(4,128)} %blocks.1) | copy-start | bytes 2116
  0.0 45.9 %copy-start.1 = (bf16[512,1024]{1,0:T(8,128)(2,1)S(1)}, bf16[512,1024]{1,0:T(8,128)(2,1)}, u32[]{:S(2)}) copy-start(bf16[512,1024]{1,0:T(8,128)(2,1)} %q_ref.1) | copy-start | bytes 3145732
  45.9 4.6 %copy-start = (bf16[24,2,4,2,128,128]{5,4,3,2,1,0:T(8,128)(2,1)S(1)}, bf16[24,2,4,2,128,128]{5,4,3,2,1,0:T(8,128)(2,1)}, u32[]{:S(2)}) copy-start(bf16[24,2,4,2,128,128]{5,4,3,2,1,0:T(8,128)(2,1)} %shard_map.55) | copy-start | bytes 37748740

commit v3 on v2

v3 whole, which is shorter than its diff:
```python
import functools

import jax
import jax.numpy as jnp
from jax import lax
from jax.experimental import pallas as pl
from jax.experimental.pallas import tpu as pltpu
from jax.sharding import PartitionSpec as P

HD = 128
HEADS = 8
BLOCK = 128
MAXB = 44
XS = 4
ZS = 8
CH = 4
GROUP_BLOCKS = 64
STEP = 4
TILE = 2 * HD
GROUPS = 16
SCALE = HD ** -0.5 * 1.4426950408889634
LIMIT = 2.0 ** 100
DEAD = 1e30
LANES = 128
VMEM_LIMIT = 60 * 2 ** 20
MESH = pl.DeviceIdType.MESH

LINKS = ("xp", "xm", "y", "zp", "zm")
STEPS = (
    {"xp": (1, 0, 0), "xm": (3, 0, 0), "y": (0, 1, 0), "zp": (0, 0, 1), "zm": (0, 0, -1)},
    {"xp": (2, 0, 0), "xm": (3, 0, 1), "y": (1, 1, 0), "zp": (1, 0, 1), "zm": (3, 0, -1)},
    {"xp": (1, 0, -1), "xm": (3, 1, 0), "y": (2, 1, 0), "zp": (0, 1, 1), "zm": (0, 1, -1)},
    {"xp": (2, 0, 1), "xm": (2, 0, -1), "y": (3, 1, 1), "zp": (1, 1, 1), "zm": (1, 1, -1)},
)
LAST = (
    (("xm", (3, 1, -1), 0), ("y", (3, 1, -1), 2), ("zp", (2, 1, 1), 1), ("zm", (2, 1, -1), 1)),
    (("xp", (2, 1, 1), 0), ("xm", (3, 1, -1), 1), ("y", (3, 1, -1), 3), ("zp", (2, 1, 1), 2), ("zm", (2, 1, -1), 2)),
    (("y", (2, 1, -1), 0), ("zp", (2, 1, 1), 3), ("zm", (2, 1, -1), 3)),
)
ORDER = ((0, 0, 0),) + tuple(row[link] for row in STEPS for link in LINKS) + ((3, 1, -1), (2, 1, 1), (2, 1, -1))
STAGES = ((0, 11, 12), (11, 16, 8), (16, 21, 8))
TICKS = CH * len(STEPS) + len(LAST)
AHEAD = 4


def parent(link, piece):
    dx, dy, dz = piece
    return {
        "xp": ((dx + XS - 1) % XS, dy, dz),
        "xm": ((dx + 1) % XS, dy, dz),
        "y": (dx, 1 - dy, dz),
        "zp": (dx, dy, dz - 1),
        "zm": (dx, dy, dz + 1),
    }[link]


def position():
    g = lax.axis_index("outer")
    inner = lax.axis_index("inner")
    cross_up = jnp.where(g % ZS == ZS - 1, 1, 0)
    cross_down = jnp.where(g % ZS == 0, 1, 0)
    return g, inner // (2 * XS), inner // 2 % XS, inner % 2, cross_up, cross_down


def nt_dot(a, b):
    return lax.dot_general(a, b, (((1,), (1,)), ((), ())), preferred_element_type=jnp.float32)


def query_tile(q_ref, row, t):
    rows = pl.ds(pl.multiple_of(row * BLOCK, BLOCK), BLOCK)
    return jnp.concatenate([q_ref[rows, h * HD:(h + 1) * HD] for h in (2 * t, 2 * t + 1)], axis=0)


def tiles():
    return [(t, pl.ds(t * TILE, TILE)) for t in range(HEADS * HD // TILE)]


def ahead(k_ref, q_ref, row, scores):
    for t, c in tiles():
        scores[:, c] = nt_dot(k_ref, query_tile(q_ref, row, t))


def attend_step(q_ref, scores, shift, total, acc, row, live, v, next_row, next_k):
    for t, c in tiles():
        base = shift[row, 0:1, c]
        parts = []
        for e in range(STEP):
            m = jnp.where(live[e], base, DEAD)
            parts.append(jnp.exp2(scores[pl.ds(e * BLOCK, BLOCK), c] * SCALE - m))
        scores[:, c] = nt_dot(next_k, query_tile(q_ref, next_row, t))
        weights = jnp.concatenate(parts, axis=0)
        total[row, :, c] += jnp.sum(weights.reshape(STEP * BLOCK // 8, 8, TILE), axis=0)
        acc[row, :, c] += jnp.dot(v, weights.astype(jnp.bfloat16), preferred_element_type=jnp.float32)


def sort_lists(blocks, counts, lists, pad, flat, table):
    g, y, x, _, cross_up, cross_down = position()
    pad[...] = jnp.zeros_like(pad)
    pad[0:lists, 0:MAXB] = blocks[...]
    block = pad[...]
    lane = lax.broadcasted_iota(jnp.int32, (8, LANES), 1)
    line = lax.broadcasted_iota(jnp.int32, (8, LANES), 0)
    length = jnp.zeros((8, LANES), jnp.int32)
    for row in range(lists):
        length = jnp.where(line == row, counts[row], length)
    group = (block // GROUP_BLOCKS - g + 1 + GROUPS) % GROUPS
    device = block % GROUP_BLOCKS // CH
    turn = jnp.where(group == 2, cross_up, jnp.where(group == 0, cross_down, 0))
    dx = (device // 2 % XS - x + XS) % XS
    dy = (device // (2 * XS) + y + turn) % 2
    code = group * 2 * XS + dy * XS + dx
    order = jnp.zeros_like(code)
    for i, (px, py, pz) in enumerate(ORDER):
        order = jnp.where(code == (pz + 1) * 2 * XS + py * XS + px, i, order)
    rank = (order * 2 + device % 2) * CH + block % CH

    def before(mask):
        ones = jnp.where(mask, 1, 0)
        count = ones
        for k in (1, 2, 4, 8, 16, 32):
            count = count + jnp.where(lane >= k, pltpu.roll(count, k, 1), 0)
        return count - ones

    rest = lane < length
    key = jnp.full((8, LANES), -1, jnp.int32)
    for kind, (first, end, slots) in enumerate(STAGES):
        mask = (lane < length) & (order >= first) & (order < end)
        place = before(mask)
        mask = mask & (place < slots)
        key = jnp.where(mask, kind * LANES + place, key)
        rest = rest & jnp.logical_not(mask)
    key = jnp.where(rest, len(STAGES) * LANES + before(rest), key)
    flat[...] = jnp.full((LANES, LANES), -1, jnp.int32)
    flat[0:8] = key
    keys = flat[...].T
    flat[0:8] = rank
    ranks = flat[...].T
    lane = lax.broadcasted_iota(jnp.int32, (LANES, LANES), 1)
    for row in range(lists):
        mine = jnp.broadcast_to(keys[:, row:row + 1], (LANES, LANES))
        value = jnp.broadcast_to(ranks[:, row:row + 1], (LANES, LANES)) + 1
        for kind in range(len(STAGES) + 1):
            line = jnp.sum(jnp.where(mine == kind * LANES + lane, value, 0), axis=0, keepdims=True)
            if kind == len(STAGES):
                left = jnp.sum(jnp.where(mine >= kind * LANES, 1, 0), axis=0, keepdims=True)
                line = jnp.where(lane[0:1] == LANES - 1, left, line)
            table[kind * 8 + row:kind * 8 + row + 1] = line


def gather_kernel(
    q_hbm, k_ref, v_ref, blocks, counts, win, acc_out, total_out, shift_out, rest_out,
    buf_a, buf_b, buf_c, q_ref, scores, shift, total, acc, pad, flat, table, slots,
    stage, side_sem, out_sem, own_sem, send_sem, recv_sem, sib_send, sib_recv,
):
    g, y, x, core, cross_up, cross_down = position()
    up, down = (g + 1) % GROUPS, (g + GROUPS - 1) % GROUPS
    lists = q_ref.shape[0] // BLOCK
    buffers = (buf_a, buf_b, buf_c)

    def place(px, py):
        return (py * XS + px) * 2 + core

    target = {
        "xp": (g, place((x + XS - 1) % XS, y)),
        "xm": (g, place((x + 1) % XS, y)),
        "y": (g, place(x, 1 - y)),
        "zp": (down, place(x, (y + cross_down) % 2)),
        "zm": (up, place(x, (y + cross_up) % 2)),
    }
    sibling = (g, (y * XS + x) * 2 + 1 - core)

    def spot(piece, side, c):
        order = ORDER.index(piece)
        for (first, end, _), buf in zip(STAGES, buffers):
            if first <= order < end:
                return buf.at[((order - first) * 2 + side) * CH + c]
        return win.at[(order * 2 + side) * CH + c]

    def at(piece, c):
        return spot(piece, core, c)

    def source(piece, c):
        return stage.at[c] if piece == ORDER[0] else at(piece, c)

    def link_copy(link, piece, c, t):
        n = LINKS.index(link)
        return pltpu.make_async_remote_copy(
            src_ref=source(parent(link, piece), c),
            dst_ref=at(piece, c),
            send_sem=send_sem.at[n, t],
            recv_sem=recv_sem.at[n, t],
            device_id=target[link],
            device_id_type=MESH,
        )

    def sib_copy(piece, c, n, t):
        return pltpu.make_async_remote_copy(
            src_ref=source(piece, c),
            dst_ref=at(piece, c),
            send_sem=sib_send.at[n, t],
            recv_sem=sib_recv.at[n, t],
            device_id=sibling,
            device_id_type=MESH,
        )

    def sib_arrival(piece, c, n, t):
        here = spot(piece, 1 - core, c)
        return pltpu.make_async_remote_copy(
            src_ref=here,
            dst_ref=here,
            send_sem=sib_send.at[n, t],
            recv_sem=sib_recv.at[n, t],
            device_id=sibling,
            device_id_type=MESH,
        )

    barrier = pltpu.get_barrier_semaphore()
    for device in (*target.values(), sibling):
        pl.semaphore_signal(barrier, inc=1, device_id=device, device_id_type=MESH)
    q_copy = pltpu.make_async_copy(q_hbm, q_ref, side_sem.at[0])
    q_copy.start()
    fill = []
    for c in range(CH):
        rows = pl.ds(c * BLOCK, BLOCK)
        stage[c, 0] = k_ref[rows]
        stage[c, 1] = v_ref[rows].T
        copy = pltpu.make_async_copy(stage.at[c], at(ORDER[0], c), own_sem.at[c])
        copy.start()
        fill.append(copy)
    pl.semaphore_wait(barrier, len(target) + 1)

    def row(step, c):
        if step < len(STEPS):
            return [(link, STEPS[step][link], c) for link in LINKS]
        return LAST[c]

    def tick(step, c):
        t = step * CH + c
        if isinstance(t, int) and t < CH:
            arrived = ()
        else:
            arrived = row(step - 1, c)
        for link, piece, chunk in arrived:
            link_copy(link, piece, chunk, t - CH).wait_recv()
        for link, piece, chunk in row(step, c) if not (step == len(STEPS) and c >= len(LAST)) else ():
            if not (isinstance(t, int) and t < AHEAD):
                link_copy(link, piece, chunk, t - AHEAD).wait_send()
            link_copy(link, piece, chunk, t).start()
        for link, piece, chunk in arrived:
            sib_copy(piece, chunk, LINKS.index(link), t - CH).start()
        if step == 0:
            sib_copy(ORDER[0], c, len(LINKS), t).start()

    for c in range(CH):
        tick(0, c)

    sort_lists(blocks, counts, lists, pad, flat, table)
    table_copy = pltpu.make_async_copy(table, slots, side_sem.at[1])
    table_copy.start()
    total[...] = jnp.zeros_like(total)
    acc[...] = jnp.zeros_like(acc)
    q_copy.wait()

    def peaks(row, _):
        own = k_ref[pl.ds(pl.multiple_of(row * BLOCK, BLOCK), BLOCK)]
        for t, c in tiles():
            s = nt_dot(own, query_tile(q_ref, row, t))
            shift[row, :, c] = jnp.broadcast_to(jnp.max(s, axis=0, keepdims=True) * SCALE, (8, TILE))
        return 0

    def early(c, _):
        tick(1, c)
        peaks(c, 0)
        return 0

    lax.fori_loop(0, CH, early, 0)
    lax.fori_loop(0, CH, lambda c, _: (tick(2, c), 0)[1], 0)
    table_copy.wait()
    for copy in fill:
        copy.wait()

    def from_sibling(step):
        def one(c, _):
            for link, piece, chunk in row(step, c):
                sib_arrival(piece, chunk, LINKS.index(link), step * CH + c).wait_recv()
            if step == 0:
                sib_arrival(ORDER[0], c, len(LINKS), c).wait_recv()
            return 0

        lax.fori_loop(0, CH, one, 0)

    exports = []

    def export(kind):
        first, end, _ = STAGES[kind]
        blocks_in = 2 * CH * (end - first)
        copy = pltpu.make_async_copy(
            buffers[kind], win.at[pl.ds(2 * CH * first, blocks_in)], out_sem.at[kind]
        )
        copy.start()
        exports.append(copy)

    def take(kind, meanwhile):
        first, _, entries = STAGES[kind]
        buf = buffers[kind]
        subs = entries // STEP

        def codes(row, sub):
            return [slots[kind * 8 + row, sub * STEP + e] for e in range(STEP)]

        def picked(code):
            return [jnp.maximum(n - 1 - 2 * CH * first, 0) for n in code]

        def keys_of(row, sub):
            return jnp.concatenate([buf[n, 0] for n in picked(codes(row, sub))], axis=0)

        ahead(keys_of(0, 0), q_ref, 0, scores)

        def one(row, _):
            meanwhile(row)
            for sub in range(subs):
                code = codes(row, sub)
                v = jnp.concatenate([buf[n, 1] for n in picked(code)], axis=1)
                if sub + 1 < subs:
                    next_row, next_sub = row, sub + 1
                else:
                    next_row, next_sub = jnp.minimum(row + 1, lists - 1), 0
                attend_step(
                    q_ref, scores, shift, total, acc, row, [n > 0 for n in code], v,
                    next_row, keys_of(next_row, next_sub),
                )
            return 0

        lax.fori_loop(0, lists, one, 0)

    from_sibling(0)
    from_sibling(1)
    export(0)
    take(0, lambda c: tick(3, c))
    from_sibling(2)
    export(1)
    for c in range(CH):
        tick(len(STEPS), c)
    take(1, lambda c: None)
    from_sibling(3)
    export(2)
    for c, last in enumerate(LAST):
        t = TICKS - len(LAST) + c
        for link, piece, chunk in last:
            link_copy(link, piece, chunk, t).wait_recv()
            sib_copy(piece, chunk, LINKS.index(link), t).start()
    take(2, lambda c: None)
    results = []
    for n, (src, dst) in enumerate(
        ((acc, acc_out), (total, total_out), (shift, shift_out), (table.at[pl.ds(8 * len(STAGES), 8)], rest_out))
    ):
        copy = pltpu.make_async_copy(src, dst, out_sem.at[len(STAGES) + n])
        copy.start()
        results.append(copy)

    sent = {link: [] for link in LINKS}
    for t in range(TICKS):
        for link, piece, chunk in row(t // CH, t % CH):
            if t >= AHEAD:
                sent[link].remove(t - AHEAD)
            sent[link].append(t)
    for link in LINKS:
        for t in sent[link]:
            link_copy(link, ORDER[1], 0, t).wait_send()

    def drain(c, _):
        for step in range(len(STEPS)):
            for link, piece, chunk in row(step, c):
                sib_copy(piece, chunk, LINKS.index(link), step * CH + c).wait_send()
        sib_copy(ORDER[0], c, len(LINKS), c).wait_send()
        return 0

    lax.fori_loop(0, CH, drain, 0)
    for c, last in enumerate(LAST):
        for link, piece, chunk in last:
            t = TICKS - len(LAST) + c
            sib_copy(piece, chunk, LINKS.index(link), t).wait_send()
            sib_arrival(piece, chunk, LINKS.index(link), t).wait_recv()


    for copy in exports + results:
        copy.wait()


def gather(queries, keys, values, blocks, counts):
    lists = queries.shape[0] // BLOCK
    rows = HEADS * BLOCK
    state = (
        jax.ShapeDtypeStruct((lists, HD, rows), jnp.float32),
        jax.ShapeDtypeStruct((lists, 8, rows), jnp.float32),
        jax.ShapeDtypeStruct((lists, 8, rows), jnp.float32),
    )
    vmem = pl.BlockSpec(memory_space=pltpu.VMEM)
    kinds = len(STAGES)
    return pl.pallas_call(
        gather_kernel,
        out_shape=(
            jax.ShapeDtypeStruct((len(ORDER) * 2 * CH, 2, BLOCK, HD), jnp.bfloat16),
            *state,
            jax.ShapeDtypeStruct((8, LANES), jnp.int32),
        ),
        in_specs=[
            pl.BlockSpec(memory_space=pl.ANY), vmem, vmem, vmem, pl.BlockSpec(memory_space=pltpu.SMEM),
        ],
        out_specs=(pl.BlockSpec(memory_space=pl.ANY),) * 5,
        scratch_shapes=[
            *(pltpu.VMEM((2 * CH * (end - first), 2, BLOCK, HD), jnp.bfloat16) for first, end, _ in STAGES),
            pltpu.VMEM(queries.shape, queries.dtype),
            pltpu.VMEM((STEP * BLOCK, rows), jnp.float32),
            pltpu.VMEM((lists, 8, rows), jnp.float32),
            pltpu.VMEM((lists, 8, rows), jnp.float32),
            pltpu.VMEM((lists, HD, rows), jnp.float32),
            pltpu.VMEM((8, LANES), jnp.int32),
            pltpu.VMEM((LANES, LANES), jnp.int32),
            pltpu.VMEM((8 * (kinds + 1), LANES), jnp.int32),
            pltpu.SMEM((8 * (kinds + 1), LANES), jnp.int32),
            pltpu.VMEM((CH, 2, BLOCK, HD), jnp.bfloat16),
            pltpu.SemaphoreType.DMA((2,)),
            pltpu.SemaphoreType.DMA((kinds + 4,)),
            pltpu.SemaphoreType.DMA((CH,)),
            pltpu.SemaphoreType.DMA((len(LINKS), TICKS)),
            pltpu.SemaphoreType.DMA((len(LINKS), TICKS)),
            pltpu.SemaphoreType.DMA((len(LINKS) + 1, TICKS)),
            pltpu.SemaphoreType.DMA((len(LINKS) + 1, TICKS)),
        ],
        compiler_params=pltpu.CompilerParams(
            collective_id=0, has_side_effects=True, vmem_limit_bytes=VMEM_LIMIT
        ),
    )(queries, keys, values, blocks, counts)


def rest_kernel(
    rest, blocks, counts, q_hbm, win, acc_hbm, total_hbm, shift_hbm, o_hbm,
    kv, q_ref, scores, shift, total, total_in, acc, acc_in, out, places, rows_of, sem, side_sem, out_sem,
):
    g, y, x, _, cross_up, cross_down = position()
    lists = q_ref.shape[0] // BLOCK
    q_copy = pltpu.make_async_copy(q_hbm, q_ref, side_sem.at[0])
    shift_copy = pltpu.make_async_copy(shift_hbm, shift, side_sem.at[1])
    total_copy = pltpu.make_async_copy(total_hbm, total_in, side_sem.at[2])
    acc_copy = pltpu.make_async_copy(acc_hbm, acc_in, side_sem.at[3])

    def fetch(n, e, source):
        return pltpu.make_async_copy(win.at[source], kv.at[n, e], sem.at[n, e])

    def plan(row, n):
        def one(s, n):
            rows_of[n, STEP] = row
            for e in range(STEP):
                code = rest[row, s * STEP + e]
                rows_of[n, e] = code
                fetch(n, e, jnp.maximum(code - 1, 0)).start()
            return n + 1

        return lax.fori_loop(0, (rest[row, LANES - 1] + STEP - 1) // STEP, one, n)

    q_copy.start()
    steps = lax.fori_loop(0, lists, plan, 0)
    for copy in (shift_copy, total_copy, acc_copy):
        copy.start()
    total[...] = jnp.zeros_like(total)
    acc[...] = jnp.zeros_like(acc)

    def wait(n):
        for e in range(STEP):
            fetch(n, e, 0).wait()

    def keys_of(n):
        return jnp.concatenate([kv[n, e, 0] for e in range(STEP)], axis=0)

    q_copy.wait()

    @pl.when(steps > 0)
    def _():
        wait(0)
        ahead(keys_of(0), q_ref, rows_of[0, STEP], scores)

    shift_copy.wait()

    def step(n, _):
        following = jnp.minimum(n + 1, steps - 1)

        @pl.when(n + 1 < steps)
        def _():
            wait(n + 1)

        v = jnp.concatenate([kv[n, e, 1] for e in range(STEP)], axis=1)
        attend_step(
            q_ref, scores, shift, total, acc, rows_of[n, STEP], [rows_of[n, e] > 0 for e in range(STEP)], v,
            rows_of[following, STEP], keys_of(following),
        )
        return 0

    lax.fori_loop(0, steps, step, 0)
    total_copy.wait()
    acc_copy.wait()

    def rank(block):
        group = (block // GROUP_BLOCKS - g + 1 + GROUPS) % GROUPS
        device = block % GROUP_BLOCKS // CH
        turn = jnp.where(group == 2, cross_up, jnp.where(group == 0, cross_down, 0))
        dx = (device // 2 % XS - x + XS) % XS
        dy = (device // (2 * XS) + y + turn) % 2
        return (places[group * 2 * XS + dy * XS + dx] * 2 + device % 2) * CH + block % CH

    def finish(row, _):
        acc[row] += acc_in[row]
        total[row] += total_in[row]
        safe = jnp.max(jnp.sum(total[row], axis=0, keepdims=True)) < LIMIT

        @pl.when(jnp.logical_not(safe))
        def _():
            for i, (dx, dy, dz) in enumerate(ORDER):
                places[(dz + 1) * 2 * XS + dy * XS + dx] = i
            for t, c in tiles():
                q = query_tile(q_ref, row, t)

                def one(e, state, q=q):
                    peak, tot, mixed = state
                    copy = fetch(0, 0, rank(blocks[row, e]))
                    copy.start()
                    copy.wait()
                    s = nt_dot(kv[0, 0, 0], q) * SCALE
                    new = jnp.maximum(peak, jnp.max(s, axis=0, keepdims=True))
                    weights = jnp.exp2(s - new)
                    keep = jnp.exp2(peak - new)
                    tot = tot * keep + jnp.sum(weights, axis=0, keepdims=True)
                    mixed = mixed * keep + jnp.dot(
                        kv[0, 0, 1], weights.astype(jnp.bfloat16), preferred_element_type=jnp.float32
                    )
                    return new, tot, mixed

                start = (
                    jnp.full((1, TILE), -DEAD, jnp.float32),
                    jnp.zeros((1, TILE), jnp.float32),
                    jnp.zeros((HD, TILE), jnp.float32),
                )
                _, tot, mixed = lax.fori_loop(0, counts[row], one, start)
                total[row, :, c] = jnp.concatenate([tot, jnp.zeros((7, TILE), jnp.float32)], axis=0)
                acc[row, :, c] = mixed

        scale = 1.0 / jnp.sum(total[row], axis=0, keepdims=True)
        rows = pl.ds(pl.multiple_of(row * BLOCK, BLOCK), BLOCK)
        for h in range(HEADS):
            c = slice(h * HD, (h + 1) * HD)
            out[rows, c] = (acc[row, :, c] * scale[:, c]).astype(jnp.bfloat16).T
        pltpu.make_async_copy(out.at[rows], o_hbm.at[rows], out_sem.at[row]).start()
        return 0

    lax.fori_loop(0, lists, finish, 0)

    def sent(row, _):
        rows = pl.ds(pl.multiple_of(row * BLOCK, BLOCK), BLOCK)
        pltpu.make_async_copy(out.at[rows], o_hbm.at[rows], out_sem.at[row]).wait()
        return 0

    lax.fori_loop(0, lists, sent, 0)


def attend_rest(rest, blocks, counts, queries, window, acc, total, shift):
    lists = queries.shape[0] // BLOCK
    steps = lists * (MAXB // STEP)
    rows = HEADS * BLOCK
    hbm = pl.BlockSpec(memory_space=pl.ANY)
    return pl.pallas_call(
        rest_kernel,
        in_specs=[pl.BlockSpec(memory_space=pltpu.SMEM)] * 3 + [hbm] * 5,
        out_specs=hbm,
        scratch_shapes=[
            pltpu.VMEM((steps, STEP, 2, BLOCK, HD), jnp.bfloat16),
            pltpu.VMEM(queries.shape, queries.dtype),
            pltpu.VMEM((STEP * BLOCK, rows), jnp.float32),
            *[pltpu.VMEM((lists, 8, rows), jnp.float32)] * 3,
            *[pltpu.VMEM((lists, HD, rows), jnp.float32)] * 2,
            pltpu.VMEM(queries.shape, queries.dtype),
            pltpu.SMEM((len(ORDER),), jnp.int32),
            pltpu.SMEM((steps, STEP + 1), jnp.int32),
            pltpu.SemaphoreType.DMA((steps, STEP)),
            pltpu.SemaphoreType.DMA((4,)),
            pltpu.SemaphoreType.DMA((lists,)),
        ],
        out_shape=jax.ShapeDtypeStruct(queries.shape, jnp.bfloat16),
        compiler_params=pltpu.CompilerParams(vmem_limit_bytes=VMEM_LIMIT),
    )(rest, blocks, counts, queries, window, acc, total, shift)


def body(queries, keys, values, key_blocks, key_counts):
    window, acc, total, shift, rest = gather(queries, keys, values, key_blocks, key_counts)
    return attend_rest(rest, key_blocks, key_counts, queries, window, acc, total, shift)


def solution(mesh):
    placed = (
        P(("outer", "inner"), None),
        P(("outer", "inner"), None),
        P(("outer", "inner"), None),
        P(("outer", "inner"), None),
        P(("outer", "inner")),
    )
    return jax.shard_map(
        body, mesh=mesh, in_specs=placed, out_specs=P(("outer", "inner"), None), check_vma=False
    )
```

time: 91.3 us -> 62.2 us (0.68)
  the two profiles are of different devices: /device:TPU:2 before, /device:TPU:5 now
where the time goes in v3:
time: 62.2 us; the launch traced here: 62.1 us
  Pallas kernels  62.1 us (100%)
    pallas_call x1, Pallas kernels, gather(): pl.pallas_call(gather_kernel, out_shape=(jax.ShapeDtypeStruct((len(ORDER)...  51.4 us
    pallas_call x1, Pallas kernels, attend_rest(): pl.pallas_call(rest_kernel, in_specs=[pl.BlockSpec(memory_space=pltpu.SME...  10.6 us

profile of v3, /device:TPU:5, one launch (start us, length us, event | category | flops | bytes accessed | tf_op | source)
XLA Modules:
  0.0 62.1 jit_solution(6387121858758772654)
XLA Ops:
  0.0 51.4 %shard_map.55 = (bf16[192,2,128,128]{3,2,1,0:T(8,128)(2,1)}, f32[4,128,1024]{2,1,0:T(8,128)}, f32[4,8,1024]{2,1,0:T(8,128)}, f32[4,8,1024]{2,1,0:T(8,128)}, s32[8,128]{1,0:T(8,128)}) custom-call(bf16[512,1024]{1,0:T(8,128)(2,1)} %q_hbm.3, bf16[512,128]{1,0:T(8,128)(2,1)} %k_ref.1, bf16[512,128]{1,0:T(8,128)(2,1)} %v_ref.1, s32[4,44]{1,0:T(4,128)} %blocks.3, ...), custom_call_target="tpu_custom_call" | custom-call | tf_op jit(solution)/shard_map/pallas_call | solution.py:400
  51.4 10.6 %shard_map.56 = bf16[512,1024]{1,0:T(8,128)(2,1)} custom-call(s32[8,128]{1,0:T(8,128)} %get-tuple-element.10.rest, s32[4,44]{1,0:T(4,128)} %blocks.3, s32[4]{0:T(128)} %counts.3, bf16[512,1024]{1,0:T(8,128)(2,1)} %q_hbm.3, bf16[192,2,128,128]{3,2,1,0:T(8,128)(2,1)} %get-tuple-element.11.win, f32[4,128,1024]{2,1,0:T(8,128)} %get-tuple-element.12.acc_hbm, ...), custom_call_target="tpu_custom_call" | custom-call | tf_op jit(solution)/shard_map/pallas_call | solution.py:570

commit v4 on v3

--- a/solution.py
+++ b/solution.py
@@ -38,7 +38,7 @@
     (("y", (2, 1, -1), 0), ("zp", (2, 1, 1), 3), ("zm", (2, 1, -1), 3)),
 )
 ORDER = ((0, 0, 0),) + tuple(row[link] for row in STEPS for link in LINKS) + ((3, 1, -1), (2, 1, 1), (2, 1, -1))
-STAGES = ((0, 11, 12), (11, 16, 8), (16, 21, 8))
+STAGES = ((0, 6, 8), (6, 11, 8), (11, 16, 8), (16, 21, 4))
 TICKS = CH * len(STEPS) + len(LAST)
 AHEAD = 4
 
@@ -148,14 +148,14 @@
 
 
 def gather_kernel(
-    q_hbm, k_ref, v_ref, blocks, counts, win, acc_out, total_out, shift_out, rest_out,
-    buf_a, buf_b, buf_c, q_ref, scores, shift, total, acc, pad, flat, table, slots,
-    stage, side_sem, out_sem, own_sem, send_sem, recv_sem, sib_send, sib_recv,
+    q_hbm, k_hbm, v_hbm, blocks, counts, win, acc_out, total_out, shift_out, rest_out,
+    buf_a, buf_b, buf_c, buf_d, q_ref, v_ref, scores, shift, total, acc, pad, flat, table, slots,
+    stage, in_sem, side_sem, out_sem, own_sem, send_sem, recv_sem, sib_send, sib_recv,
 ):
     g, y, x, core, cross_up, cross_down = position()
     up, down = (g + 1) % GROUPS, (g + GROUPS - 1) % GROUPS
     lists = q_ref.shape[0] // BLOCK
-    buffers = (buf_a, buf_b, buf_c)
+    buffers = (buf_a, buf_b, buf_c, buf_d)
 
     def place(px, py):
         return (py * XS + px) * 2 + core
@@ -169,62 +169,61 @@
     }
     sibling = (g, (y * XS + x) * 2 + 1 - core)
 
-    def spot(piece, side, c):
-        order = ORDER.index(piece)
+    def part(order, side, c, blocks):
         for (first, end, _), buf in zip(STAGES, buffers):
             if first <= order < end:
-                return buf.at[((order - first) * 2 + side) * CH + c]
-        return win.at[(order * 2 + side) * CH + c]
+                return buf.at[pl.ds(((order - first) * 2 + side) * CH + c, blocks)]
+        return win.at[pl.ds((order * 2 + side) * CH + c, blocks)]
 
     def at(piece, c):
-        return spot(piece, core, c)
+        return part(ORDER.index(piece), core, c, 1)
 
     def source(piece, c):
-        return stage.at[c] if piece == ORDER[0] else at(piece, c)
+        return stage.at[pl.ds(c, 1)] if piece == ORDER[0] else at(piece, c)
+
+    def remote(src, dst, send, recv, device):
+        return pltpu.make_async_remote_copy(
+            src_ref=src, dst_ref=dst, send_sem=send, recv_sem=recv, device_id=device, device_id_type=MESH
+        )
 
     def link_copy(link, piece, c, t):
-        n = LINKS.index(link)
-        return pltpu.make_async_remote_copy(
-            src_ref=source(parent(link, piece), c),
-            dst_ref=at(piece, c),
-            send_sem=send_sem.at[n, t],
-            recv_sem=recv_sem.at[n, t],
-            device_id=target[link],
-            device_id_type=MESH,
+        return remote(
+            source(parent(link, piece), c), at(piece, c), send_sem.at[t], recv_sem.at[t], target[link]
         )
 
-    def sib_copy(piece, c, n, t):
-        return pltpu.make_async_remote_copy(
-            src_ref=source(piece, c),
-            dst_ref=at(piece, c),
-            send_sem=sib_send.at[n, t],
-            recv_sem=sib_recv.at[n, t],
-            device_id=sibling,
-            device_id_type=MESH,
-        )
-
-    def sib_arrival(piece, c, n, t):
-        here = spot(piece, 1 - core, c)
-        return pltpu.make_async_remote_copy(
-            src_ref=here,
-            dst_ref=here,
-            send_sem=sib_send.at[n, t],
-            recv_sem=sib_recv.at[n, t],
-            device_id=sibling,
-            device_id_type=MESH,
-        )
+    def sib_copy(piece, c, n, blocks):
+        side = core
+        order = ORDER.index(piece)
+        if piece == ORDER[0]:
+            src = stage.at[pl.ds(c, blocks)]
+        else:
+            src = part(order, side, c, blocks)
+        return remote(src, part(order, side, c, blocks), sib_send.at[n], sib_recv.at[n], sibling)
+
+    def many(blocks, sems, n):
+        some = buf_a.at[pl.ds(0, blocks)]
+        return remote(some, some, sems[0].at[n], sems[1].at[n], sibling)
+
+    links, sibs = (send_sem, recv_sem), (sib_send, sib_recv)
+    last_sib = 1 + 2 * len(STEPS)
 
     barrier = pltpu.get_barrier_semaphore()
     for device in (*target.values(), sibling):
         pl.semaphore_signal(barrier, inc=1, device_id=device, device_id_type=MESH)
+    k_copies, v_copies, fill = [], [], []
+    for c in range(CH):
+        rows = pl.ds(c * BLOCK, BLOCK)
+        k_copies.append(pltpu.make_async_copy(k_hbm.at[rows], stage.at[c, 0], in_sem.at[0, c]))
+        v_copies.append(pltpu.make_async_copy(v_hbm.at[rows], v_ref.at[c], in_sem.at[1, c]))
+        k_copies[c].start()
+        v_copies[c].start()
     q_copy = pltpu.make_async_copy(q_hbm, q_ref, side_sem.at[0])
     q_copy.start()
-    fill = []
     for c in range(CH):
-        rows = pl.ds(c * BLOCK, BLOCK)
-        stage[c, 0] = k_ref[rows]
-        stage[c, 1] = v_ref[rows].T
-        copy = pltpu.make_async_copy(stage.at[c], at(ORDER[0], c), own_sem.at[c])
+        v_copies[c].wait()
+        stage[c, 1] = v_ref[c].T
+        k_copies[c].wait()
+        copy = pltpu.make_async_copy(stage.at[pl.ds(c, 1)], at(ORDER[0], c), own_sem.at[c])
         copy.start()
         fill.append(copy)
     pl.semaphore_wait(barrier, len(target) + 1)
@@ -234,25 +233,38 @@
             return [(link, STEPS[step][link], c) for link in LINKS]
         return LAST[c]
 
+    def when(condition, run):
+        if isinstance(condition, bool):
+            if condition:
+                run()
+        else:
+            pl.when(condition)(run)
+
     def tick(step, c):
         t = step * CH + c
-        if isinstance(t, int) and t < CH:
-            arrived = ()
-        else:
-            arrived = row(step - 1, c)
-        for link, piece, chunk in arrived:
-            link_copy(link, piece, chunk, t - CH).wait_recv()
-        for link, piece, chunk in row(step, c) if not (step == len(STEPS) and c >= len(LAST)) else ():
-            if not (isinstance(t, int) and t < AHEAD):
-                link_copy(link, piece, chunk, t - AHEAD).wait_send()
-            link_copy(link, piece, chunk, t).start()
-        for link, piece, chunk in arrived:
-            sib_copy(piece, chunk, LINKS.index(link), t - CH).start()
-        if step == 0:
-            sib_copy(ORDER[0], c, len(LINKS), t).start()
+        now = row(step, c) if step < len(STEPS) or c < len(LAST) else ()
+        late = [step == 1 or (link == "y" and step == 2) for link, _, _ in now]
+        if now and step * CH >= AHEAD:
+            if step < len(STEPS) or not isinstance(t, int):
+                many(len(LINKS), links, t - AHEAD).wait_send()
+            else:
+                many(len(row((t - AHEAD) // CH, (t - AHEAD) % CH)), links, t - AHEAD).wait_send()
+        for after in (False, True):
+            if after and step > 0:
+                many(len(LINKS), links, t - CH).wait_recv()
+            for (link, piece, chunk), tardy in zip(now, late):
+                if tardy == after:
+                    link_copy(link, piece, chunk, t).start()
+        if step > 0:
+            def forward():
+                for link, piece, _ in row(step - 1, c):
+                    sib_copy(piece, c - 1, 1 + 2 * (step - 1) + c // 2, 2).start()
+
+            when(c % 2 == 1, forward)
 
     for c in range(CH):
         tick(0, c)
+    sib_copy(ORDER[0], 0, 0, CH).start()
 
     sort_lists(blocks, counts, lists, pad, flat, table)
     table_copy = pltpu.make_async_copy(table, slots, side_sem.at[1])
@@ -262,7 +274,7 @@
     q_copy.wait()
 
     def peaks(row, _):
-        own = k_ref[pl.ds(pl.multiple_of(row * BLOCK, BLOCK), BLOCK)]
+        own = stage[row, 0]
         for t, c in tiles():
             s = nt_dot(own, query_tile(q_ref, row, t))
             shift[row, :, c] = jnp.broadcast_to(jnp.max(s, axis=0, keepdims=True) * SCALE, (8, TILE))
@@ -274,20 +286,15 @@
         return 0
 
     lax.fori_loop(0, CH, early, 0)
-    lax.fori_loop(0, CH, lambda c, _: (tick(2, c), 0)[1], 0)
     table_copy.wait()
     for copy in fill:
         copy.wait()
 
     def from_sibling(step):
-        def one(c, _):
-            for link, piece, chunk in row(step, c):
-                sib_arrival(piece, chunk, LINKS.index(link), step * CH + c).wait_recv()
-            if step == 0:
-                sib_arrival(ORDER[0], c, len(LINKS), c).wait_recv()
-            return 0
-
-        lax.fori_loop(0, CH, one, 0)
+        if step == 0:
+            many(CH, sibs, 0).wait_recv()
+        for half in range(2):
+            many(2 * len(LINKS), sibs, 1 + 2 * step + half).wait_recv()
 
     exports = []
 
@@ -333,23 +340,17 @@
 
         lax.fori_loop(0, lists, one, 0)
 
-    from_sibling(0)
-    from_sibling(1)
-    export(0)
-    take(0, lambda c: tick(3, c))
-    from_sibling(2)
-    export(1)
-    for c in range(CH):
-        tick(len(STEPS), c)
-    take(1, lambda c: None)
-    from_sibling(3)
-    export(2)
-    for c, last in enumerate(LAST):
-        t = TICKS - len(LAST) + c
-        for link, piece, chunk in last:
-            link_copy(link, piece, chunk, t).wait_recv()
-            sib_copy(piece, chunk, LINKS.index(link), t).start()
-    take(2, lambda c: None)
+    for kind in range(len(STAGES)):
+        from_sibling(kind)
+        export(kind)
+        if kind + 2 < len(STAGES):
+            take(kind, lambda c, kind=kind: tick(kind + 2, c))
+        elif kind + 2 == len(STAGES):
+            for c in range(CH):
+                tick(len(STEPS), c)
+            take(kind, lambda c: None)
+        else:
+            take(kind, lambda c: None)
     results = []
     for n, (src, dst) in enumerate(
         ((acc, acc_out), (total, total_out), (shift, shift_out), (table.at[pl.ds(8 * len(STAGES), 8)], rest_out))
@@ -358,31 +359,18 @@
         copy.start()
         results.append(copy)
 
-    sent = {link: [] for link in LINKS}
-    for t in range(TICKS):
-        for link, piece, chunk in row(t // CH, t % CH):
-            if t >= AHEAD:
-                sent[link].remove(t - AHEAD)
-            sent[link].append(t)
-    for link in LINKS:
-        for t in sent[link]:
-            link_copy(link, ORDER[1], 0, t).wait_send()
-
-    def drain(c, _):
-        for step in range(len(STEPS)):
-            for link, piece, chunk in row(step, c):
-                sib_copy(piece, chunk, LINKS.index(link), step * CH + c).wait_send()
-        sib_copy(ORDER[0], c, len(LINKS), c).wait_send()
-        return 0
-
-    lax.fori_loop(0, CH, drain, 0)
     for c, last in enumerate(LAST):
+        many(len(last), links, len(STEPS) * CH + c).wait_recv()
         for link, piece, chunk in last:
-            t = TICKS - len(LAST) + c
-            sib_copy(piece, chunk, LINKS.index(link), t).wait_send()
-            sib_arrival(piece, chunk, LINKS.index(link), t).wait_recv()
-
-
+            sib_copy(piece, chunk, last_sib + c, 1).start()
+    for t in range(TICKS - AHEAD, TICKS):
+        many(len(row(t // CH, t % CH)), links, t).wait_send()
+    many(CH, sibs, 0).wait_send()
+    for n in range(1, last_sib):
+        many(2 * len(LINKS), sibs, n).wait_send()
+    for c, last in enumerate(LAST):
+        many(len(last), sibs, last_sib + c).wait_send()
+        many(len(last), sibs, last_sib + c).wait_recv()
     for copy in exports + results:
         copy.wait()
 
@@ -405,12 +393,13 @@
             jax.ShapeDtypeStruct((8, LANES), jnp.int32),
         ),
         in_specs=[
-            pl.BlockSpec(memory_space=pl.ANY), vmem, vmem, vmem, pl.BlockSpec(memory_space=pltpu.SMEM),
+            *[pl.BlockSpec(memory_space=pl.ANY)] * 3, vmem, pl.BlockSpec(memory_space=pltpu.SMEM),
         ],
         out_specs=(pl.BlockSpec(memory_space=pl.ANY),) * 5,
         scratch_shapes=[
             *(pltpu.VMEM((2 * CH * (end - first), 2, BLOCK, HD), jnp.bfloat16) for first, end, _ in STAGES),
             pltpu.VMEM(queries.shape, queries.dtype),
+            pltpu.VMEM((CH, BLOCK, HD), jnp.bfloat16),
             pltpu.VMEM((STEP * BLOCK, rows), jnp.float32),
             pltpu.VMEM((lists, 8, rows), jnp.float32),
             pltpu.VMEM((lists, 8, rows), jnp.float32),
@@ -420,13 +409,14 @@
             pltpu.VMEM((8 * (kinds + 1), LANES), jnp.int32),
             pltpu.SMEM((8 * (kinds + 1), LANES), jnp.int32),
             pltpu.VMEM((CH, 2, BLOCK, HD), jnp.bfloat16),
+            pltpu.SemaphoreType.DMA((2, CH)),
             pltpu.SemaphoreType.DMA((2,)),
             pltpu.SemaphoreType.DMA((kinds + 4,)),
             pltpu.SemaphoreType.DMA((CH,)),
-            pltpu.SemaphoreType.DMA((len(LINKS), TICKS)),
-            pltpu.SemaphoreType.DMA((len(LINKS), TICKS)),
-            pltpu.SemaphoreType.DMA((len(LINKS) + 1, TICKS)),
-            pltpu.SemaphoreType.DMA((len(LINKS) + 1, TICKS)),
+            pltpu.SemaphoreType.DMA((TICKS,)),
+            pltpu.SemaphoreType.DMA((TICKS,)),
+            pltpu.SemaphoreType.DMA((1 + 2 * len(STEPS) + len(LAST),)),
+            pltpu.SemaphoreType.DMA((1 + 2 * len(STEPS) + len(LAST),)),
         ],
         compiler_params=pltpu.CompilerParams(
             collective_id=0, has_side_effects=True, vmem_limit_bytes=VMEM_LIMIT
@@ -435,36 +425,34 @@
 
 
 def rest_kernel(
-    rest, blocks, counts, q_hbm, win, acc_hbm, total_hbm, shift_hbm, o_hbm,
-    kv, q_ref, scores, shift, total, total_in, acc, acc_in, out, places, rows_of, sem, side_sem, out_sem,
+    rest, blocks_hbm, counts_hbm, q_hbm, win, acc_hbm, total_hbm, shift_hbm, o_hbm,
+    kv, q_ref, scores, shift, total, acc, out, blocks, counts, places, plan, sem, side_sem, out_sem,
 ):
     g, y, x, _, cross_up, cross_down = position()
     lists = q_ref.shape[0] // BLOCK
     q_copy = pltpu.make_async_copy(q_hbm, q_ref, side_sem.at[0])
     shift_copy = pltpu.make_async_copy(shift_hbm, shift, side_sem.at[1])
-    total_copy = pltpu.make_async_copy(total_hbm, total_in, side_sem.at[2])
-    acc_copy = pltpu.make_async_copy(acc_hbm, acc_in, side_sem.at[3])
+    total_copy = pltpu.make_async_copy(total_hbm, total, side_sem.at[2])
+    acc_copy = pltpu.make_async_copy(acc_hbm, acc, side_sem.at[3])
 
     def fetch(n, e, source):
         return pltpu.make_async_copy(win.at[source], kv.at[n, e], sem.at[n, e])
 
-    def plan(row, n):
+    def plan_list(row, n):
         def one(s, n):
-            rows_of[n, STEP] = row
+            plan[n, STEP] = row
             for e in range(STEP):
                 code = rest[row, s * STEP + e]
-                rows_of[n, e] = code
+                plan[n, e] = code
                 fetch(n, e, jnp.maximum(code - 1, 0)).start()
             return n + 1
 
         return lax.fori_loop(0, (rest[row, LANES - 1] + STEP - 1) // STEP, one, n)
 
     q_copy.start()
-    steps = lax.fori_loop(0, lists, plan, 0)
+    steps = lax.fori_loop(0, lists, plan_list, 0)
     for copy in (shift_copy, total_copy, acc_copy):
         copy.start()
-    total[...] = jnp.zeros_like(total)
-    acc[...] = jnp.zeros_like(acc)
 
     def wait(n):
         for e in range(STEP):
@@ -478,9 +466,10 @@
     @pl.when(steps > 0)
     def _():
         wait(0)
-        ahead(keys_of(0), q_ref, rows_of[0, STEP], scores)
-
-    shift_copy.wait()
+        ahead(keys_of(0), q_ref, plan[0, STEP], scores)
+
+    for copy in (shift_copy, total_copy, acc_copy):
+        copy.wait()
 
     def step(n, _):
         following = jnp.minimum(n + 1, steps - 1)
@@ -491,14 +480,12 @@
 
         v = jnp.concatenate([kv[n, e, 1] for e in range(STEP)], axis=1)
         attend_step(
-            q_ref, scores, shift, total, acc, rows_of[n, STEP], [rows_of[n, e] > 0 for e in range(STEP)], v,
-            rows_of[following, STEP], keys_of(following),
+            q_ref, scores, shift, total, acc, plan[n, STEP], [plan[n, e] > 0 for e in range(STEP)], v,
+            plan[following, STEP], keys_of(following),
         )
         return 0
 
     lax.fori_loop(0, steps, step, 0)
-    total_copy.wait()
-    acc_copy.wait()
 
     def rank(block):
         group = (block // GROUP_BLOCKS - g + 1 + GROUPS) % GROUPS
@@ -508,42 +495,48 @@
         dy = (device // (2 * XS) + y + turn) % 2
         return (places[group * 2 * XS + dy * XS + dx] * 2 + device % 2) * CH + block % CH
 
+    def again(row, _):
+        for t, c in tiles():
+            q = query_tile(q_ref, row, t)
+
+            def one(e, state, q=q):
+                peak, tot, mixed = state
+                copy = fetch(0, 0, rank(blocks[row, e]))
+                copy.start()
+                copy.wait()
+                s = nt_dot(kv[0, 0, 0], q) * SCALE
+                new = jnp.maximum(peak, jnp.max(s, axis=0, keepdims=True))
+                weights = jnp.exp2(s - new)
+                keep = jnp.exp2(peak - new)
+                tot = tot * keep + jnp.sum(weights, axis=0, keepdims=True)
+                mixed = mixed * keep + jnp.dot(
+                    kv[0, 0, 1], weights.astype(jnp.bfloat16), preferred_element_type=jnp.float32
+                )
+                return new, tot, mixed
+
+            start = (
+                jnp.full((1, TILE), -DEAD, jnp.float32),
+                jnp.zeros((1, TILE), jnp.float32),
+                jnp.zeros((HD, TILE), jnp.float32),
+            )
+            _, tot, mixed = lax.fori_loop(0, counts[row], one, start)
+            total[row, :, c] = jnp.concatenate([tot, jnp.zeros((7, TILE), jnp.float32)], axis=0)
+            acc[row, :, c] = mixed
+        return 0
+
+    safe = jnp.max(jnp.sum(total[...], axis=1)) < LIMIT
+
+    @pl.when(jnp.logical_not(safe))
+    def _():
+        for n, (src, dst) in enumerate(((blocks_hbm, blocks), (counts_hbm, counts))):
+            copy = pltpu.make_async_copy(src, dst, side_sem.at[n])
+            copy.start()
+            copy.wait()
+        for i, (dx, dy, dz) in enumerate(ORDER):
+            places[(dz + 1) * 2 * XS + dy * XS + dx] = i
+        lax.fori_loop(0, lists, again, 0)
+
     def finish(row, _):
-        acc[row] += acc_in[row]
-        total[row] += total_in[row]
-        safe = jnp.max(jnp.sum(total[row], axis=0, keepdims=True)) < LIMIT
-
-        @pl.when(jnp.logical_not(safe))
-        def _():
-            for i, (dx, dy, dz) in enumerate(ORDER):
-                places[(dz + 1) * 2 * XS + dy * XS + dx] = i
-            for t, c in tiles():
-                q = query_tile(q_ref, row, t)
-
-                def one(e, state, q=q):
-                    peak, tot, mixed = state
-                    copy = fetch(0, 0, rank(blocks[row, e]))
-                    copy.start()
-                    copy.wait()
-                    s = nt_dot(kv[0, 0, 0], q) * SCALE
-                    new = jnp.maximum(peak, jnp.max(s, axis=0, keepdims=True))
-                    weights = jnp.exp2(s - new)
-                    keep = jnp.exp2(peak - new)
-                    tot = tot * keep + jnp.sum(weights, axis=0, keepdims=True)
-                    mixed = mixed * keep + jnp.dot(
-                        kv[0, 0, 1], weights.astype(jnp.bfloat16), preferred_element_type=jnp.float32
-                    )
-                    return new, tot, mixed
-
-                start = (
-                    jnp.full((1, TILE), -DEAD, jnp.float32),
-                    jnp.zeros((1, TILE), jnp.float32),
-                    jnp.zeros((HD, TILE), jnp.float32),
-                )
-                _, tot, mixed = lax.fori_loop(0, counts[row], one, start)
-                total[row, :, c] = jnp.concatenate([tot, jnp.zeros((7, TILE), jnp.float32)], axis=0)
-                acc[row, :, c] = mixed
-
         scale = 1.0 / jnp.sum(total[row], axis=0, keepdims=True)
         rows = pl.ds(pl.multiple_of(row * BLOCK, BLOCK), BLOCK)
         for h in range(HEADS):
@@ -569,15 +562,17 @@
     hbm = pl.BlockSpec(memory_space=pl.ANY)
     return pl.pallas_call(
         rest_kernel,
-        in_specs=[pl.BlockSpec(memory_space=pltpu.SMEM)] * 3 + [hbm] * 5,
+        in_specs=[pl.BlockSpec(memory_space=pltpu.SMEM)] + [hbm] * 7,
         out_specs=hbm,
         scratch_shapes=[
             pltpu.VMEM((steps, STEP, 2, BLOCK, HD), jnp.bfloat16),
             pltpu.VMEM(queries.shape, queries.dtype),
             pltpu.VMEM((STEP * BLOCK, rows), jnp.float32),
-            *[pltpu.VMEM((lists, 8, rows), jnp.float32)] * 3,
-            *[pltpu.VMEM((lists, HD, rows), jnp.float32)] * 2,
+            *[pltpu.VMEM((lists, 8, rows), jnp.float32)] * 2,
+            pltpu.VMEM((lists, HD, rows), jnp.float32),
             pltpu.VMEM(queries.shape, queries.dtype),
+            pltpu.SMEM(blocks.shape, jnp.int32),
+            pltpu.SMEM(counts.shape, jnp.int32),
             pltpu.SMEM((len(ORDER),), jnp.int32),
             pltpu.SMEM((steps, STEP + 1), jnp.int32),
             pltpu.SemaphoreType.DMA((steps, STEP)),

time: 62.2 us -> 58.9 us (0.947)
  the two profiles are of different devices: /device:TPU:5 before, /device:TPU:7 now
where the time goes in v4:
time: 58.9 us; the launch traced here: 58.7 us
  Pallas kernels  58.7 us (100%)
    pallas_call x1, Pallas kernels, gather(): pl.pallas_call(gather_kernel, out_shape=(jax.ShapeDtypeStruct((len(ORDER)...  47.3 us
    pallas_call x1, Pallas kernels, attend_rest(): pl.pallas_call(rest_kernel, in_specs=[pl.BlockSpec(memory_space=pltpu.SME...  11.4 us

profile of v4, /device:TPU:7, one launch (start us, length us, event | category | flops | bytes accessed | tf_op | source)
XLA Modules:
  0.0 58.7 jit_solution(2006839226680421233)
XLA Ops:
  0.0 47.3 %shard_map.55 = (bf16[192,2,128,128]{3,2,1,0:T(8,128)(2,1)}, f32[4,128,1024]{2,1,0:T(8,128)}, f32[4,8,1024]{2,1,0:T(8,128)}, f32[4,8,1024]{2,1,0:T(8,128)}, s32[8,128]{1,0:T(8,128)}) custom-call(bf16[512,1024]{1,0:T(8,128)(2,1)} %q_hbm.3, bf16[512,128]{1,0:T(8,128)(2,1)} %k_hbm.1, bf16[512,128]{1,0:T(8,128)(2,1)} %v_hbm.1, s32[4,44]{1,0:T(4,128)} %blocks_hbm.1, ...), custom_call_target="tpu_custom_call" | custom-call | tf_op jit(solution)/shard_map/pallas_call | solution.py:388
  47.3 11.4 %shard_map.56 = bf16[512,1024]{1,0:T(8,128)(2,1)} custom-call(s32[8,128]{1,0:T(8,128)} %get-tuple-element.10.rest, s32[4,44]{1,0:T(4,128)} %blocks_hbm.1, s32[4]{0:T(128)} %counts_hbm.1, bf16[512,1024]{1,0:T(8,128)(2,1)} %q_hbm.3, bf16[192,2,128,128]{3,2,1,0:T(8,128)(2,1)} %get-tuple-element.11.win, f32[4,128,1024]{2,1,0:T(8,128)} %get-tuple-element.12.acc_hbm, ...), custom_call_target="tpu_custom_call" | custom-call | tf_op jit(solution)/shard_map/pallas_call | solution.py:563

commit v5 on v4

--- a/solution.py
+++ b/solution.py
@@ -16,6 +16,7 @@
 CH = 4
 GROUP_BLOCKS = 64
 STEP = 4
+PART = 2
 TILE = 2 * HD
 GROUPS = 16
 SCALE = HD ** -0.5 * 1.4426950408889634
@@ -75,21 +76,22 @@
     return [(t, pl.ds(t * TILE, TILE)) for t in range(HEADS * HD // TILE)]
 
 
-def ahead(k_ref, q_ref, row, scores):
+def ahead(k, q_ref, row, scores, first=0):
     for t, c in tiles():
-        scores[:, c] = nt_dot(k_ref, query_tile(q_ref, row, t))
-
-
-def attend_step(q_ref, scores, shift, total, acc, row, live, v, next_row, next_k):
+        scores[pl.ds(first, k.shape[0]), c] = nt_dot(k, query_tile(q_ref, row, t))
+
+
+def attend_step(q_ref, scores, shift, total, acc, row, live, v, next_row, next_k, first=0):
+    keys = len(live) * BLOCK
     for t, c in tiles():
         base = shift[row, 0:1, c]
         parts = []
-        for e in range(STEP):
+        for e in range(len(live)):
             m = jnp.where(live[e], base, DEAD)
-            parts.append(jnp.exp2(scores[pl.ds(e * BLOCK, BLOCK), c] * SCALE - m))
-        scores[:, c] = nt_dot(next_k, query_tile(q_ref, next_row, t))
+            parts.append(jnp.exp2(scores[pl.ds(first + e * BLOCK, BLOCK), c] * SCALE - m))
+        scores[pl.ds(first, keys), c] = nt_dot(next_k, query_tile(q_ref, next_row, t))
         weights = jnp.concatenate(parts, axis=0)
-        total[row, :, c] += jnp.sum(weights.reshape(STEP * BLOCK // 8, 8, TILE), axis=0)
+        total[row, :, c] += jnp.sum(weights.reshape(keys // 8, 8, TILE), axis=0)
         acc[row, :, c] += jnp.dot(v, weights.astype(jnp.bfloat16), preferred_element_type=jnp.float32)
 
 
@@ -307,7 +309,17 @@
         copy.start()
         exports.append(copy)
 
-    def take(kind, meanwhile):
+    results = []
+
+    def deliver(pairs):
+        for src, dst in pairs:
+            copy = pltpu.make_async_copy(src, dst, out_sem.at[len(STAGES) + len(results)])
+            copy.start()
+            results.append(copy)
+
+    deliver(((shift, shift_out), (table.at[pl.ds(8 * len(STAGES), 8)], rest_out)))
+
+    def take(kind, meanwhile, unrolled=False):
         first, _, entries = STAGES[kind]
         buf = buffers[kind]
         subs = entries // STEP
@@ -331,14 +343,26 @@
                 if sub + 1 < subs:
                     next_row, next_sub = row, sub + 1
                 else:
-                    next_row, next_sub = jnp.minimum(row + 1, lists - 1), 0
+                    next_row, next_sub = row + 1, 0
+                    next_row = min(next_row, lists - 1) if unrolled else jnp.minimum(next_row, lists - 1)
                 attend_step(
                     q_ref, scores, shift, total, acc, row, [n > 0 for n in code], v,
                     next_row, keys_of(next_row, next_sub),
                 )
+            if kind + 1 == len(STAGES):
+                deliver(((acc.at[row], acc_out.at[row]), (total.at[row], total_out.at[row])))
             return 0
 
-        lax.fori_loop(0, lists, one, 0)
+        if unrolled:
+            for row in range(lists):
+                one(row, 0)
+        else:
+            lax.fori_loop(0, lists, one, 0)
+
+    def last_arrival(c):
+        many(len(LAST[c]), links, len(STEPS) * CH + c).wait_recv()
+        for link, piece, chunk in LAST[c]:
+            sib_copy(piece, chunk, last_sib + c, 1).start()
 
     for kind in range(len(STAGES)):
         from_sibling(kind)
@@ -346,23 +370,9 @@
         if kind + 2 < len(STAGES):
             take(kind, lambda c, kind=kind: tick(kind + 2, c))
         elif kind + 2 == len(STAGES):
-            for c in range(CH):
-                tick(len(STEPS), c)
-            take(kind, lambda c: None)
+            take(kind, lambda c: tick(len(STEPS), c), True)
         else:
-            take(kind, lambda c: None)
-    results = []
-    for n, (src, dst) in enumerate(
-        ((acc, acc_out), (total, total_out), (shift, shift_out), (table.at[pl.ds(8 * len(STAGES), 8)], rest_out))
-    ):
-        copy = pltpu.make_async_copy(src, dst, out_sem.at[len(STAGES) + n])
-        copy.start()
-        results.append(copy)
-
-    for c, last in enumerate(LAST):
-        many(len(last), links, len(STEPS) * CH + c).wait_recv()
-        for link, piece, chunk in last:
-            sib_copy(piece, chunk, last_sib + c, 1).start()
+            take(kind, lambda c: last_arrival(c - 1) if c > 0 else None, True)
     for t in range(TICKS - AHEAD, TICKS):
         many(len(row(t // CH, t % CH)), links, t).wait_send()
     many(CH, sibs, 0).wait_send()
@@ -411,7 +421,7 @@
             pltpu.VMEM((CH, 2, BLOCK, HD), jnp.bfloat16),
             pltpu.SemaphoreType.DMA((2, CH)),
             pltpu.SemaphoreType.DMA((2,)),
-            pltpu.SemaphoreType.DMA((kinds + 4,)),
+            pltpu.SemaphoreType.DMA((kinds + 2 + 2 * lists,)),
             pltpu.SemaphoreType.DMA((CH,)),
             pltpu.SemaphoreType.DMA((TICKS,)),
             pltpu.SemaphoreType.DMA((TICKS,)),
@@ -425,8 +435,8 @@
 
 
 def rest_kernel(
-    rest, blocks_hbm, counts_hbm, q_hbm, win, acc_hbm, total_hbm, shift_hbm, o_hbm,
-    kv, q_ref, scores, shift, total, acc, out, blocks, counts, places, plan, sem, side_sem, out_sem,
+    rest_hbm, blocks_hbm, counts_hbm, q_hbm, win, acc_hbm, total_hbm, shift_hbm, o_hbm,
+    kv, q_ref, scores, shift, total, acc, out, rest, blocks, counts, places, plan, sem, side_sem, out_sem,
 ):
     g, y, x, _, cross_up, cross_down = position()
     lists = q_ref.shape[0] // BLOCK
@@ -438,35 +448,48 @@
     def fetch(n, e, source):
         return pltpu.make_async_copy(win.at[source], kv.at[n, e], sem.at[n, e])
 
+    def plan_part(n, row, codes):
+        plan[n, PART] = row
+        for e, code in enumerate(codes):
+            plan[n, e] = code
+            fetch(n, e, jnp.maximum(code - 1, 0)).start()
+
     def plan_list(row, n):
         def one(s, n):
-            plan[n, STEP] = row
-            for e in range(STEP):
-                code = rest[row, s * STEP + e]
-                plan[n, e] = code
-                fetch(n, e, jnp.maximum(code - 1, 0)).start()
+            plan_part(n, row, [rest[row, s * PART + e] for e in range(PART)])
             return n + 1
 
-        return lax.fori_loop(0, (rest[row, LANES - 1] + STEP - 1) // STEP, one, n)
-
-    q_copy.start()
-    steps = lax.fori_loop(0, lists, plan_list, 0)
-    for copy in (shift_copy, total_copy, acc_copy):
+        return lax.fori_loop(0, (rest[row, LANES - 1] + PART - 1) // PART, one, n)
+
+    rest_copy = pltpu.make_async_copy(rest_hbm, rest, side_sem.at[4])
+    for copy in (rest_copy, q_copy, shift_copy):
         copy.start()
+    rest_copy.wait()
+    parts = lax.fori_loop(0, lists, plan_list, 0)
+
+    @pl.when(parts % 2 == 1)
+    def _():
+        plan_part(parts, 0, [0] * PART)
+
+    steps = (parts + 1) // 2
+    for copy in (total_copy, acc_copy):
+        copy.start()
 
     def wait(n):
-        for e in range(STEP):
-            fetch(n, e, 0).wait()
+        for e in range(PART):
+            fetch(2 * n, e, 0).wait()
+            fetch(2 * n + 1, e, 0).wait()
 
     def keys_of(n):
-        return jnp.concatenate([kv[n, e, 0] for e in range(STEP)], axis=0)
+        return jnp.concatenate([kv[n, e, 0] for e in range(PART)], axis=0)
 
     q_copy.wait()
 
     @pl.when(steps > 0)
     def _():
         wait(0)
-        ahead(keys_of(0), q_ref, plan[0, STEP], scores)
+        for n in range(2):
+            ahead(keys_of(n), q_ref, plan[n, PART], scores, n * PART * BLOCK)
 
     for copy in (shift_copy, total_copy, acc_copy):
         copy.wait()
@@ -478,11 +501,13 @@
         def _():
             wait(n + 1)
 
-        v = jnp.concatenate([kv[n, e, 1] for e in range(STEP)], axis=1)
-        attend_step(
-            q_ref, scores, shift, total, acc, plan[n, STEP], [plan[n, e] > 0 for e in range(STEP)], v,
-            plan[following, STEP], keys_of(following),
-        )
+        for half in range(2):
+            now, later = 2 * n + half, 2 * following + half
+            v = jnp.concatenate([kv[now, e, 1] for e in range(PART)], axis=1)
+            attend_step(
+                q_ref, scores, shift, total, acc, plan[now, PART], [plan[now, e] > 0 for e in range(PART)], v,
+                plan[later, PART], keys_of(later), half * PART * BLOCK,
+            )
         return 0
 
     lax.fori_loop(0, steps, step, 0)
@@ -557,26 +582,27 @@
 
 def attend_rest(rest, blocks, counts, queries, window, acc, total, shift):
     lists = queries.shape[0] // BLOCK
-    steps = lists * (MAXB // STEP)
+    parts = lists * (MAXB // PART)
     rows = HEADS * BLOCK
     hbm = pl.BlockSpec(memory_space=pl.ANY)
     return pl.pallas_call(
         rest_kernel,
-        in_specs=[pl.BlockSpec(memory_space=pltpu.SMEM)] + [hbm] * 7,
+        in_specs=[hbm] * 8,
         out_specs=hbm,
         scratch_shapes=[
-            pltpu.VMEM((steps, STEP, 2, BLOCK, HD), jnp.bfloat16),
+            pltpu.VMEM((parts, PART, 2, BLOCK, HD), jnp.bfloat16),
             pltpu.VMEM(queries.shape, queries.dtype),
             pltpu.VMEM((STEP * BLOCK, rows), jnp.float32),
             *[pltpu.VMEM((lists, 8, rows), jnp.float32)] * 2,
             pltpu.VMEM((lists, HD, rows), jnp.float32),
             pltpu.VMEM(queries.shape, queries.dtype),
+            pltpu.SMEM(rest.shape, jnp.int32),
             pltpu.SMEM(blocks.shape, jnp.int32),
             pltpu.SMEM(counts.shape, jnp.int32),
             pltpu.SMEM((len(ORDER),), jnp.int32),
-            pltpu.SMEM((steps, STEP + 1), jnp.int32),
-            pltpu.SemaphoreType.DMA((steps, STEP)),
-            pltpu.SemaphoreType.DMA((4,)),
+            pltpu.SMEM((parts, PART + 1), jnp.int32),
+            pltpu.SemaphoreType.DMA((parts, PART)),
+            pltpu.SemaphoreType.DMA((5,)),
             pltpu.SemaphoreType.DMA((lists,)),
         ],
         out_shape=jax.ShapeDtypeStruct(queries.shape, jnp.bfloat16),

time: 58.9 us -> 53 us (0.90)
  the two profiles are of different devices: /device:TPU:7 before, /device:TPU:1 now
where the time goes in v5:
time: 53 us; the launch traced here: 52.8 us
  Pallas kernels  52.6 us (99%)
    pallas_call x1, Pallas kernels, gather(): pl.pallas_call(gather_kernel, out_shape=(jax.ShapeDtypeStruct((len(ORDER)...  44.3 us
    pallas_call x1, Pallas kernels, attend_rest(): pl.pallas_call(rest_kernel, in_specs=[hbm] * 8, out_specs=hbm, scratch_sh...  8.33 us

profile of v5, /device:TPU:1, one launch (start us, length us, event | category | flops | bytes accessed | tf_op | source)
XLA Modules:
  0.0 52.8 jit_solution(13290063711306072317)
XLA Ops:
  0.0 44.3 %shard_map.55 = (bf16[192,2,128,128]{3,2,1,0:T(8,128)(2,1)}, f32[4,128,1024]{2,1,0:T(8,128)}, f32[4,8,1024]{2,1,0:T(8,128)}, f32[4,8,1024]{2,1,0:T(8,128)}, s32[8,128]{1,0:T(8,128)}) custom-call(bf16[512,1024]{1,0:T(8,128)(2,1)} %q_hbm.3, bf16[512,128]{1,0:T(8,128)(2,1)} %k_hbm.1, bf16[512,128]{1,0:T(8,128)(2,1)} %v_hbm.1, s32[4,44]{1,0:T(4,128)} %blocks_hbm.1, ...), custom_call_target="tpu_custom_call" | custom-call | tf_op jit(solution)/shard_map/pallas_call | solution.py:398
  44.3 8.3 %shard_map.56 = bf16[512,1024]{1,0:T(8,128)(2,1)} custom-call(s32[8,128]{1,0:T(8,128)} %get-tuple-element.10.rest_hbm, s32[4,44]{1,0:T(4,128)} %blocks_hbm.1, s32[4]{0:T(128)} %counts_hbm.1, bf16[512,1024]{1,0:T(8,128)(2,1)} %q_hbm.3, bf16[192,2,128,128]{3,2,1,0:T(8,128)(2,1)} %get-tuple-element.11.win, f32[4,128,1024]{2,1,0:T(8,128)} %get-tuple-element.12.acc_hbm, ...), custom_call_target="tpu_custom_call" | custom-call | tf_op jit(solution)/shard_map/pallas_call | solution.py:588

commit v6 on v5

--- a/solution.py
+++ b/solution.py
@@ -34,9 +34,11 @@
     {"xp": (2, 0, 1), "xm": (2, 0, -1), "y": (3, 1, 1), "zp": (1, 1, 1), "zm": (1, 1, -1)},
 )
 LAST = (
-    (("xm", (3, 1, -1), 0), ("y", (3, 1, -1), 2), ("zp", (2, 1, 1), 1), ("zm", (2, 1, -1), 1)),
-    (("xp", (2, 1, 1), 0), ("xm", (3, 1, -1), 1), ("y", (3, 1, -1), 3), ("zp", (2, 1, 1), 2), ("zm", (2, 1, -1), 2)),
-    (("y", (2, 1, -1), 0), ("zp", (2, 1, 1), 3), ("zm", (2, 1, -1), 3)),
+    (("xm", (3, 1, -1), 0, None), ("y", (3, 1, -1), 3, None), ("zm", (2, 1, -1), 3, None), ("zp", (2, 1, 1), 3, None),
+     ("xp", (2, 1, 1), 0, None)),
+    (("xm", (3, 1, -1), 1, None), ("y", (3, 1, -1), 2, None), ("zm", (2, 1, -1), 2, None), ("zp", (2, 1, 1), 2, None),
+     ("xp", (2, 1, -1), 0, None)),
+    (("xm", (2, 1, 1), 1, 1), ("xp", (2, 1, -1), 1, 1), ("zm", (2, 1, -1), 1, 0), ("zp", (2, 1, 1), 1, 0)),
 )
 ORDER = ((0, 0, 0),) + tuple(row[link] for row in STEPS for link in LINKS) + ((3, 1, -1), (2, 1, 1), (2, 1, -1))
 STAGES = ((0, 6, 8), (6, 11, 8), (11, 16, 8), (16, 21, 4))
@@ -123,10 +125,10 @@
             count = count + jnp.where(lane >= k, pltpu.roll(count, k, 1), 0)
         return count - ones
 
-    rest = lane < length
+    rest = (lane > 0) & (lane < length)
     key = jnp.full((8, LANES), -1, jnp.int32)
     for kind, (first, end, slots) in enumerate(STAGES):
-        mask = (lane < length) & (order >= first) & (order < end)
+        mask = (lane > 0) & (lane < length) & (order >= first) & (order < end)
         place = before(mask)
         mask = mask & (place < slots)
         key = jnp.where(mask, kind * LANES + place, key)
@@ -177,21 +179,25 @@
                 return buf.at[pl.ds(((order - first) * 2 + side) * CH + c, blocks)]
         return win.at[pl.ds((order * 2 + side) * CH + c, blocks)]
 
-    def at(piece, c):
-        return part(ORDER.index(piece), core, c, 1)
-
-    def source(piece, c):
-        return stage.at[pl.ds(c, 1)] if piece == ORDER[0] else at(piece, c)
+    def at(piece, c, half=None):
+        chunk = part(ORDER.index(piece), core, c, 1)
+        return chunk if half is None else chunk.at[0, half]
+
+    def source(piece, c, half=None):
+        return stage.at[pl.ds(c, 1)] if piece == ORDER[0] else at(piece, c, half)
 
     def remote(src, dst, send, recv, device):
         return pltpu.make_async_remote_copy(
             src_ref=src, dst_ref=dst, send_sem=send, recv_sem=recv, device_id=device, device_id_type=MESH
         )
 
-    def link_copy(link, piece, c, t):
+    def link_copy(link, piece, c, half, t):
         return remote(
-            source(parent(link, piece), c), at(piece, c), send_sem.at[t], recv_sem.at[t], target[link]
+            source(parent(link, piece), c, half), at(piece, c, half), send_sem.at[t], recv_sem.at[t], target[link]
         )
+
+    def chunks(items):
+        return sum(2 if half is None else 1 for _, _, _, half in items) // 2
 
     def sib_copy(piece, c, n, blocks):
         side = core
@@ -221,18 +227,18 @@
         v_copies[c].start()
     q_copy = pltpu.make_async_copy(q_hbm, q_ref, side_sem.at[0])
     q_copy.start()
-    for c in range(CH):
+
+    def ready(c):
         v_copies[c].wait()
         stage[c, 1] = v_ref[c].T
         k_copies[c].wait()
-        copy = pltpu.make_async_copy(stage.at[pl.ds(c, 1)], at(ORDER[0], c), own_sem.at[c])
-        copy.start()
-        fill.append(copy)
+
+    ready(0)
     pl.semaphore_wait(barrier, len(target) + 1)
 
     def row(step, c):
         if step < len(STEPS):
-            return [(link, STEPS[step][link], c) for link in LINKS]
+            return [(link, STEPS[step][link], c, None) for link in LINKS]
         return LAST[c]
 
     def when(condition, run):
@@ -245,46 +251,57 @@
     def tick(step, c):
         t = step * CH + c
         now = row(step, c) if step < len(STEPS) or c < len(LAST) else ()
-        late = [step == 1 or (link == "y" and step == 2) for link, _, _ in now]
+        late = [
+            step == 1 or (step, link) == (2, "y") or (step == len(STEPS) and (c, link) == (0, "xp"))
+            for link, _, _, _ in now
+        ]
         if now and step * CH >= AHEAD:
             if step < len(STEPS) or not isinstance(t, int):
                 many(len(LINKS), links, t - AHEAD).wait_send()
             else:
-                many(len(row((t - AHEAD) // CH, (t - AHEAD) % CH)), links, t - AHEAD).wait_send()
+                many(chunks(row((t - AHEAD) // CH, (t - AHEAD) % CH)), links, t - AHEAD).wait_send()
         for after in (False, True):
             if after and step > 0:
                 many(len(LINKS), links, t - CH).wait_recv()
-            for (link, piece, chunk), tardy in zip(now, late):
+            for item, tardy in zip(now, late):
                 if tardy == after:
-                    link_copy(link, piece, chunk, t).start()
+                    link_copy(*item, t).start()
         if step > 0:
             def forward():
-                for link, piece, _ in row(step - 1, c):
+                for _, piece, _, _ in row(step - 1, c):
                     sib_copy(piece, c - 1, 1 + 2 * (step - 1) + c // 2, 2).start()
 
             when(c % 2 == 1, forward)
 
     for c in range(CH):
+        if c > 0:
+            ready(c)
         tick(0, c)
     sib_copy(ORDER[0], 0, 0, CH).start()
+    for c in range(CH):
+        copy = pltpu.make_async_copy(stage.at[pl.ds(c, 1)], at(ORDER[0], c), own_sem.at[c])
+        copy.start()
+        fill.append(copy)
 
     sort_lists(blocks, counts, lists, pad, flat, table)
     table_copy = pltpu.make_async_copy(table, slots, side_sem.at[1])
     table_copy.start()
-    total[...] = jnp.zeros_like(total)
-    acc[...] = jnp.zeros_like(acc)
     q_copy.wait()
 
-    def peaks(row, _):
-        own = stage[row, 0]
+    def attend_own(row):
         for t, c in tiles():
-            s = nt_dot(own, query_tile(q_ref, row, t))
-            shift[row, :, c] = jnp.broadcast_to(jnp.max(s, axis=0, keepdims=True) * SCALE, (8, TILE))
-        return 0
+            s = nt_dot(stage[row, 0], query_tile(q_ref, row, t)) * SCALE
+            peak = jnp.max(s, axis=0, keepdims=True)
+            shift[row, :, c] = jnp.broadcast_to(peak, (8, TILE))
+            weights = jnp.exp2(s - peak)
+            total[row, :, c] = jnp.sum(weights.reshape(BLOCK // 8, 8, TILE), axis=0)
+            acc[row, :, c] = jnp.dot(
+                stage[row, 1], weights.astype(jnp.bfloat16), preferred_element_type=jnp.float32
+            )
 
     def early(c, _):
         tick(1, c)
-        peaks(c, 0)
+        attend_own(c)
         return 0
 
     lax.fori_loop(0, CH, early, 0)
@@ -360,9 +377,10 @@
             lax.fori_loop(0, lists, one, 0)
 
     def last_arrival(c):
-        many(len(LAST[c]), links, len(STEPS) * CH + c).wait_recv()
-        for link, piece, chunk in LAST[c]:
-            sib_copy(piece, chunk, last_sib + c, 1).start()
+        many(chunks(LAST[c]), links, len(STEPS) * CH + c).wait_recv()
+        for _, piece, chunk, half in LAST[c]:
+            ref = at(piece, chunk, half)
+            remote(ref, ref, sib_send.at[last_sib + c], sib_recv.at[last_sib + c], sibling).start()
 
     for kind in range(len(STAGES)):
         from_sibling(kind)
@@ -374,13 +392,13 @@
         else:
             take(kind, lambda c: last_arrival(c - 1) if c > 0 else None, True)
     for t in range(TICKS - AHEAD, TICKS):
-        many(len(row(t // CH, t % CH)), links, t).wait_send()
+        many(chunks(row(t // CH, t % CH)), links, t).wait_send()
     many(CH, sibs, 0).wait_send()
     for n in range(1, last_sib):
         many(2 * len(LINKS), sibs, n).wait_send()
     for c, last in enumerate(LAST):
-        many(len(last), sibs, last_sib + c).wait_send()
-        many(len(last), sibs, last_sib + c).wait_recv()
+        many(chunks(last), sibs, last_sib + c).wait_send()
+        many(chunks(last), sibs, last_sib + c).wait_recv()
     for copy in exports + results:
         copy.wait()
 
@@ -462,7 +480,7 @@
         return lax.fori_loop(0, (rest[row, LANES - 1] + PART - 1) // PART, one, n)
 
     rest_copy = pltpu.make_async_copy(rest_hbm, rest, side_sem.at[4])
-    for copy in (rest_copy, q_copy, shift_copy):
+    for copy in (rest_copy, q_copy, shift_copy, total_copy, acc_copy):
         copy.start()
     rest_copy.wait()
     parts = lax.fori_loop(0, lists, plan_list, 0)
@@ -472,8 +490,6 @@
         plan_part(parts, 0, [0] * PART)
 
     steps = (parts + 1) // 2
-    for copy in (total_copy, acc_copy):
-        copy.start()
 
     def wait(n):
         for e in range(PART):

time: 53 us -> 53.9 us (1.017)
    pallas_call x1, Pallas kernels: 8.33 us -> 9.25 us  [attend_rest(): pl.pallas_call(rest_kernel, in_specs=[hbm] * 8, out_specs=hbm, scratch_sh...]
where the time goes in v6:
time: 53.9 us; the launch traced here: 53.2 us
  Pallas kernels  53 us (98%)
    pallas_call x1, Pallas kernels, gather(): pl.pallas_call(gather_kernel, out_shape=(jax.ShapeDtypeStruct((len(ORDER)...  43.8 us
    pallas_call x1, Pallas kernels, attend_rest(): pl.pallas_call(rest_kernel, in_specs=[hbm] * 8, out_specs=hbm, scratch_sh...  9.25 us

profile of v6, /device:TPU:1, one launch (start us, length us, event | category | flops | bytes accessed | tf_op | source)
XLA Modules:
  0.0 53.2 jit_solution(9478824779690786566)
XLA Ops:
  0.0 43.8 %shard_map.55 = (bf16[192,2,128,128]{3,2,1,0:T(8,128)(2,1)}, f32[4,128,1024]{2,1,0:T(8,128)}, f32[4,8,1024]{2,1,0:T(8,128)}, f32[4,8,1024]{2,1,0:T(8,128)}, s32[8,128]{1,0:T(8,128)}) custom-call(bf16[512,1024]{1,0:T(8,128)(2,1)} %q_hbm.3, bf16[512,128]{1,0:T(8,128)(2,1)} %k_hbm.1, bf16[512,128]{1,0:T(8,128)(2,1)} %v_hbm.1, s32[4,44]{1,0:T(4,128)} %blocks_hbm.1, ...), custom_call_target="tpu_custom_call" | custom-call | tf_op jit(solution)/shard_map/pallas_call | solution.py:416
  43.8 9.2 %shard_map.56 = bf16[512,1024]{1,0:T(8,128)(2,1)} custom-call(s32[8,128]{1,0:T(8,128)} %get-tuple-element.10.rest_hbm, s32[4,44]{1,0:T(4,128)} %blocks_hbm.1, s32[4]{0:T(128)} %counts_hbm.1, bf16[512,1024]{1,0:T(8,128)(2,1)} %q_hbm.3, bf16[192,2,128,128]{3,2,1,0:T(8,128)(2,1)} %get-tuple-element.11.win, f32[4,128,1024]{2,1,0:T(8,128)} %get-tuple-element.12.acc_hbm, ...), custom_call_target="tpu_custom_call" | custom-call | tf_op jit(solution)/shard_map/pallas_call | solution.py:604
